TPU v7x, 256 devices: a whole 4x4x8 slice. The times are simulated.
256 devices in a mesh: dp: 32 (over x_hi, z, core), expert: 8 (over x_lo, y).
Axes of the slice: x: 4 (x_hi: 2, x_lo: 2; x = x_hi * 2 + x_lo), y: 4, z: 8, core: 2. Of those that a mesh axis runs over, the one named last changes fastest.
Arguments:
- tokens: bfloat16 [32768, 2048], P(('dp', 'expert')), may hold values from -24 to 24
- cotangent: bfloat16 [32768, 2048], P(('dp', 'expert')), may hold values from -6 to 6
- probs: bfloat16 [32768, 2], P(('dp', 'expert')), may hold values from 0.19921875 to 1
- routes: int32 [32768, 2], P(('dp', 'expert')), may hold values from 0 to 7, all different within a row; in each aligned block of 128 rows (0 to 127, 128 to 255, ...) at most 40 rows name the same one
- live: int32 [512], P(('dp', 'expert')), may hold values 0 or 1
- slot_map: int32 [8], replicated, may hold values from 0 to 7, each once
- w_gate: bfloat16 [8, 2048, 768], P('expert'), may hold values from -0.125 to 0.125
- w_up: bfloat16 [8, 2048, 768], P('expert'), may hold values from -0.125 to 0.125
- w_down: bfloat16 [8, 768, 2048], P('expert'), may hold values from -0.21875 to 0.21875
Outputs:
- input_grad: bfloat16 [32768, 2048], P(('dp', 'expert'))
- prob_grad: bfloat16 [32768, 2], P(('dp', 'expert'))
- grad_gate: float32 [8, 2048, 768], P('expert', 'dp')
- grad_up: float32 [8, 2048, 768], P('expert', 'dp')
- grad_down: float32 [8, 768, 2048], P('expert', None, 'dp')
Inputs may be any that keep to these rules, and one draw needn't show every extreme that they name: `routes`: the tokens of one device name each expert in at most 40 pairs; some expert reaches 40 on some device. `slot_map`: each slot is named once.
All inputs are finite; a program needn't handle non-finite values. No bound on the sum of `live` on one device may be relied on, other than what follows from the above.
Results may differ from a plain program's by a relative error of at most 0.019.
Values may be sent and summed in bfloat16 or wider, within the bound.
A program may use at most 128 MiB of HBM per device.

v0:
```python
import jax
import jax.numpy as jnp
from jax import lax
from jax.sharding import PartitionSpec as P


def contract_rows(left, right):
    return lax.dot_general(
        left, right, (((0,), (0,)), ((), ())), preferred_element_type=jnp.float32
    )


def contract_cols(left, right):
    return lax.dot_general(
        left, right, (((1,), (1,)), ((), ())), preferred_element_type=jnp.float32
    )


def shards(tokens, cotangent, probs, routes, live, slot_map, w_gate, w_up, w_down):
    rows, top = routes.shape
    width = tokens.shape[1]
    groups = lax.axis_size("expert")
    experts = slot_map.shape[0]
    cap = min(rows, rows * top * 5 // (4 * experts))
    slots = groups * cap
    alive = jnp.repeat(live, rows // live.shape[0])
    chosen = routes[:, :, None] == jnp.arange(experts, dtype=jnp.int32)[None, None, :]
    owner = jnp.sum(jnp.where(chosen, slot_map[None, None, :], 0), -1).reshape(-1)
    pair_live = jnp.repeat(alive, top) == 1
    taken = (
        (owner[:, None] == jnp.arange(groups, dtype=jnp.int32)[None, :]) & pair_live[:, None]
    ).astype(jnp.int32)
    before = jnp.cumsum(taken, 0) - taken
    position = jnp.sum(before * taken, 1)
    target = jnp.where(pair_live, owner * cap + position, -1)
    pick = (target[None, :] == jnp.arange(slots, dtype=jnp.int32)[:, None]).astype(jnp.float32)
    by_token = jnp.sum(pick.reshape(slots, rows, top), 2).astype(jnp.bfloat16)
    send_x = (
        jnp.dot(by_token, tokens, preferred_element_type=jnp.float32)
        .astype(jnp.bfloat16)
        .reshape(groups, cap, width)
    )
    send_dy = (
        jnp.dot(by_token, cotangent, preferred_element_type=jnp.float32)
        .astype(jnp.bfloat16)
        .reshape(groups, cap, width)
    )
    send_p = (
        jnp.sum(pick * probs.reshape(-1).astype(jnp.float32)[None, :], 1)
        .astype(jnp.bfloat16)
        .reshape(groups, cap)
    )
    gate_w = w_gate[0]
    up_w = w_up[0]
    down_w = w_down[0]
    got_x, got_p = (
        lax.all_to_all(send_x, "expert", split_axis=0, concat_axis=0, tiled=True),
        lax.all_to_all(send_p, "expert", split_axis=0, concat_axis=0, tiled=True),
    )
    rows_x = got_x.reshape(slots, width)
    gate = jnp.dot(rows_x, gate_w, preferred_element_type=jnp.float32)
    up = jnp.dot(rows_x, up_w, preferred_element_type=jnp.float32)
    got_dy = lax.all_to_all(send_dy, "expert", split_axis=0, concat_axis=0, tiled=True)
    rows_dy = got_dy.reshape(slots, width)
    weight = got_p.reshape(slots).astype(jnp.float32)
    sig = jax.nn.sigmoid(gate)
    hidden = (gate * sig * up).astype(jnp.bfloat16)
    expert_out = jnp.dot(hidden, down_w, preferred_element_type=jnp.float32)
    prob_part = jnp.sum(expert_out * rows_dy.astype(jnp.float32), -1).astype(jnp.bfloat16)
    scaled = (weight[:, None] * rows_dy.astype(jnp.float32)).astype(jnp.bfloat16)
    grad_down = contract_rows(hidden, scaled)
    hidden_grad = contract_cols(scaled, down_w)
    gate_grad = (hidden_grad * up * sig * (1.0 + gate * (1.0 - sig))).astype(jnp.bfloat16)
    up_grad = (hidden_grad * gate * sig).astype(jnp.bfloat16)
    pair = (contract_cols(gate_grad, gate_w) + contract_cols(up_grad, up_w)).astype(jnp.bfloat16)
    back, back_p = (
        lax.all_to_all(
            pair.reshape(groups, cap, width), "expert", split_axis=0, concat_axis=0, tiled=True
        ),
        lax.all_to_all(
            prob_part.reshape(groups, cap), "expert", split_axis=0, concat_axis=0, tiled=True
        ),
    )
    grad_gate = contract_rows(rows_x, gate_grad)
    grad_up = contract_rows(rows_x, up_grad)
    gate_share, up_share, down_share = (
        lax.psum_scatter(
            grad_gate[None].astype(jnp.bfloat16), "dp", scatter_dimension=1, tiled=True
        ).astype(jnp.float32),
        lax.psum_scatter(
            grad_up[None].astype(jnp.bfloat16), "dp", scatter_dimension=1, tiled=True
        ).astype(jnp.float32),
        lax.psum_scatter(
            grad_down[None].astype(jnp.bfloat16), "dp", scatter_dimension=2, tiled=True
        ).astype(jnp.float32),
    )
    input_grad = contract_rows(by_token, back.reshape(slots, width)).astype(jnp.bfloat16)
    prob_grad = (
        jnp.sum(pick * back_p.reshape(slots).astype(jnp.float32)[:, None], 0)
        .reshape(rows, top)
        .astype(jnp.bfloat16)
    )
    return (input_grad, prob_grad, gate_share, up_share, down_share)


def solution(mesh):
    return jax.shard_map(
        shards,
        mesh=mesh,
        in_specs=(
            P(("dp", "expert"), None),
            P(("dp", "expert"), None),
            P(("dp", "expert"), None),
            P(("dp", "expert"), None),
            P(("dp", "expert")),
            P(),
            P("expert", None, None),
            P("expert", None, None),
            P("expert", None, None),
        ),
        out_specs=(
            P(("dp", "expert"), None),
            P(("dp", "expert"), None),
            P("expert", "dp", None),
            P("expert", "dp", None),
            P("expert", None, "dp"),
        ),
        check_vma=False,
    )
```

profile of v0, /device:TPU:24, one launch (start us, length us, event | category | flops | bytes accessed | tf_op | source)
XLA Modules:
  0.0 491.0 jit_solution(16958029054165999624)
XLA Ops:
  7.2 0.9 select_reduce_fusion.2
  8.1 0.1 copy.31
  8.2 0.1 eq.92
  8.4 0.1 eq.97
  8.5 0.7 broadcast_compare_fusion
  9.2 0.1 broadcast_in_dim.22
  9.2 0.1 eq.88
  9.3 0.1 broadcast_in_dim.23.clone
  9.4 0.1 eq.96
  9.6 0.1 fusion.32
  9.7 0.6 reduce-window.6
  10.2 0.2 slice_reduce_fusion
  10.5 0.1 fusion.29
  10.6 0.1 reduce_sum.58
  10.7 0.1 copy.34
  10.8 0.1 convert_reduce_fusion
  10.9 2.6 convolution_convert_fusion.3
  13.5 6.1 %all-to-all-start.2 = ((bf16[8,40,2048]{2,1,0:T(8,128)(2,1)}), bf16[8,40,2048]{2,1,0:T(8,128)(2,1)}, u32[]{:S(2)}, u32[]{:S(2)}) async-start(bf16[8,40,2048]{2,1,0:T(8,128)(2,1)} %bitcast.76), calls=%async_computation.2 | async-start | bytes 2621440 | tf_op jit(solution)/shard_map/all_to_all | solution.py:57
  19.6 2.6 convolution_convert_fusion.4
  22.2 12.9 %all-to-all-done.2 = bf16[8,40,2048]{2,1,0:T(8,128)(2,1)} async-done(((bf16[8,40,2048]{2,1,0:T(8,128)(2,1)}), bf16[8,40,2048]{2,1,0:T(8,128)(2,1)}, u32[]{:S(2)}, u32[]{:S(2)}) %all-to-all-start.2) | async-done | bytes 1310752 | tf_op jit(solution)/shard_map/all_to_all | solution.py:57
  35.1 5.9 %all-to-all-start.1 = ((bf16[8,40,2048]{2,1,0:T(8,128)(2,1)}), bf16[8,40,2048]{2,1,0:T(8,128)(2,1)}, u32[]{:S(2)}, u32[]{:S(2)}) async-start(bf16[8,40,2048]{2,1,0:T(8,128)(2,1)} %bitcast.75), calls=%async_computation.1 | async-start | bytes 2621440 | tf_op jit(solution)/shard_map/all_to_all | solution.py:63
  41.0 3.5 fusion.2
  44.5 1.0 copy-done.2
  45.4 3.6 multiply_convert_fusion.3
  49.0 8.2 %all-to-all-done.1 = bf16[8,40,2048]{2,1,0:T(8,128)(2,1)} async-done(((bf16[8,40,2048]{2,1,0:T(8,128)(2,1)}), bf16[8,40,2048]{2,1,0:T(8,128)(2,1)}, u32[]{:S(2)}, u32[]{:S(2)}) %all-to-all-start.1) | async-done | bytes 1310752 | tf_op jit(solution)/shard_map/all_to_all | solution.py:63
  57.2 3.7 fusion.24
  60.9 0.7 convert_element_type.196
  61.6 5.2 %all-to-all-start.4 = ((bf16[8,1,40]{2,1,0:T(2,128)(2,1)}), bf16[8,1,40]{2,1,0:T(2,128)(2,1)S(1)}, u32[]{:S(2)}, u32[]{:S(2)}) async-start(bf16[8,1,40]{2,1,0:T(2,128)(2,1)} %convert_element_type.196), calls=%async_computation.4 | async-start | bytes 8192 | tf_op jit(solution)/shard_map/all_to_all | solution.py:80
  66.8 0.1 copy.35
  67.0 0.1 reshape.170
  67.1 3.7 all-to-all-done.4
  70.8 0.1 reshape.173
  70.9 0.2 select_reduce_fusion
  71.2 0.1 convert_element_type.195
  71.2 8.5 %all_to_all.27 = bf16[8,1,40]{2,1,0:T(2,128)(2,1)S(1)} all-to-all(bf16[8,1,40]{2,1,0:T(2,128)(2,1)S(1)} %convert_element_type.195), channel_id=1, replica_groups=mesh['dp'=32,'expert'=8] {'expert'}, dimensions={0} | all-to-all | bytes 1280 | tf_op jit(solution)/shard_map/all_to_all | solution.py:58
  79.8 0.1 reshape.174
  79.9 5.1 %fusion.14 = bf16[1,768,2048]{2,1,0:T(8,128)(2,1)} fusion(bf16[320,768]{1,0:T(8,128)(2,1)} %get-tuple-element.34, f32[320]{0:T(512)S(1)} %reshape.174, bf16[320,2048]{1,0:T(8,128)(2,1)} %bitcast.50), kind=kOutput, calls=%fused_computation.18 | convolution fusion | flops 1010171904 | bytes 4949248 | tf_op jit(solution)/shard_map/dot_general | solution.py:8
  84.9 15.7 %copy.40 = bf16[1,768,2048]{1,0,2:T(2,128)(2,1)} copy(bf16[1,768,2048]{2,1,0:T(8,128)(2,1)} %fusion.14) | data formatting | bytes 6291456
  100.7 5.0 %copy.44 = bf16[2048,1,768]{2,0,1:T(8,128)(2,1)} copy(bf16[2048,1,768]{2,1,0:T(2,128)(2,1)} %bitcast.73) | data formatting | bytes 6291456
  105.7 0.0 reduce-scatter.10.cloned.1.call-update
  105.7 0.0 reduce-scatter.8.cloned.1.call-start
  105.8 1.7 multiply_convert_fusion.1
  107.5 0.1 copy-done.6
  107.6 4.2 multiply_convert_fusion.4
  111.9 0.8 copy-done.4
  112.7 4.9 fusion.13
  117.5 0.0 reduce-scatter.8.cloned.1.call-update
  117.5 0.2 reduce-scatter.6.cloned.1.call-start
  117.8 5.0 %fusion.12 = bf16[1,2048,768]{2,1,0:T(8,128)(2,1)} fusion(bf16[320,2048]{1,0:T(8,128)(2,1)} %bitcast.7, bf16[320,768]{1,0:T(8,128)(2,1)} %get-tuple-element.33), kind=kOutput, calls=%fused_computation.16 | convolution fusion | flops 1008205824 | bytes 4947968 | tf_op jit(solution)/shard_map/dot_general | solution.py:8
  122.8 3.4 fusion
  126.2 2.3 fusion.21
  128.5 6.2 %all-to-all-start.3 = ((bf16[8,40,2048]{2,1,0:T(8,128)(2,1)}), bf16[8,40,2048]{2,1,0:T(8,128)(2,1)}, u32[]{:S(2)}, u32[]{:S(2)}) async-start(bf16[8,40,2048]{2,1,0:T(8,128)(2,1)} %bitcast.77), calls=%async_computation.3 | async-start | bytes 2621440 | tf_op jit(solution)/shard_map/all_to_all | solution.py:77
  134.7 0.2 convert_element_type.177
  134.9 0.6 copy.38
  135.5 13.2 %all-to-all-done.3 = bf16[8,40,2048]{2,1,0:T(8,128)(2,1)} async-done(((bf16[8,40,2048]{2,1,0:T(8,128)(2,1)}), bf16[8,40,2048]{2,1,0:T(8,128)(2,1)}, u32[]{:S(2)}, u32[]{:S(2)}) %all-to-all-start.3) | async-done | bytes 1310752 | tf_op jit(solution)/shard_map/all_to_all | solution.py:77
  148.7 2.6 convolution_convert_fusion.5
  151.3 80.1 %reduce-scatter.10.cloned.1.call-done = bf16[64,768]{1,0:T(8,128)(2,1)} async-done(((bf16[2048,768]{1,0:T(8,128)(2,1)}), bf16[64,768]{1,0:T(8,128)(2,1)}) %reduce-scatter.10.cloned.1.call-update) | async-done | bytes 98320
  231.4 1.0 reshape_bitcast_fusion
  232.4 0.2 copy.41
  232.6 0.8 copy.39
  233.4 124.1 %reduce-scatter.8.cloned.1.call-done = bf16[1,64,768]{2,1,0:T(8,128)(2,1)} async-done(((bf16[1,2048,768]{2,1,0:T(8,128)(2,1)}), bf16[1,64,768]{2,1,0:T(8,128)(2,1)}) %reduce-scatter.8.cloned.1.call-update) | async-done | bytes 98320 | tf_op jit(solution)/shard_map/reduce_scatter | solution.py:90
  357.5 1.6 convert_element_type.183
  359.0 123.8 %reduce-scatter.6.cloned.1.call-done = bf16[1,64,768]{2,1,0:T(8,128)(2,1)} async-done(((bf16[1,2048,768]{2,1,0:T(8,128)(2,1)}), bf16[1,64,768]{2,1,0:T(8,128)(2,1)}) %reduce-scatter.6.cloned.1.call-update) | async-done | bytes 98320 | tf_op jit(solution)/shard_map/reduce_scatter | solution.py:87
  482.9 1.6 convert_element_type.180
  (20 shorter events, 0.1 us)
Async XLA Ops:
  7.2 38.2 %copy-start = (bf16[1,2048,768]{2,1,0:T(8,128)(2,1)S(1)}, bf16[1,2048,768]{2,1,0:T(8,128)(2,1)}, u32[]{:S(2)}) copy-start(bf16[1,2048,768]{2,1,0:T(8,128)(2,1)} %param.16) | copy-start | bytes 9437188
  13.5 21.6 %all-to-all-start.2 = ((bf16[8,40,2048]{2,1,0:T(8,128)(2,1)}), bf16[8,40,2048]{2,1,0:T(8,128)(2,1)}, u32[]{:S(2)}, u32[]{:S(2)}) async-start(bf16[8,40,2048]{2,1,0:T(8,128)(2,1)} %bitcast.76), calls=%async_computation.2 | async-start | bytes 2621440 | tf_op jit(solution)/shard_map/all_to_all | solution.py:57
  35.1 22.1 %all-to-all-start.1 = ((bf16[8,40,2048]{2,1,0:T(8,128)(2,1)}), bf16[8,40,2048]{2,1,0:T(8,128)(2,1)}, u32[]{:S(2)}, u32[]{:S(2)}) async-start(bf16[8,40,2048]{2,1,0:T(8,128)(2,1)} %bitcast.75), calls=%async_computation.1 | async-start | bytes 2621440 | tf_op jit(solution)/shard_map/all_to_all | solution.py:63
  44.4 1.0 copy-start.2
  57.2 9.6 %copy-start.1 = (bf16[128,2]{0,1:T(2,128)(2,1)S(1)}, bf16[128,2]{0,1:T(2,128)(2,1)}, u32[]{:S(2)}) copy-start(bf16[128,2]{0,1:T(2,128)(2,1)} %param.11) | copy-start | bytes 1540
  61.6 9.2 %all-to-all-start.4 = ((bf16[8,1,40]{2,1,0:T(2,128)(2,1)}), bf16[8,1,40]{2,1,0:T(2,128)(2,1)S(1)}, u32[]{:S(2)}, u32[]{:S(2)}) async-start(bf16[8,1,40]{2,1,0:T(2,128)(2,1)} %convert_element_type.196), calls=%async_computation.4 | async-start | bytes 8192 | tf_op jit(solution)/shard_map/all_to_all | solution.py:80
  66.8 164.5 %reduce-scatter.10.cloned.1.call-start = ((), (), s32[]{:S(2)}) async-start(), calls=%async_computation.10 | async-start | bytes 3244032
  105.7 251.8 %reduce-scatter.8.cloned.1.call-start = ((), (), s32[]{:S(2)}) async-start(), calls=%async_computation.9 | async-start | bytes 3244032 | tf_op jit(solution)/shard_map/reduce_scatter | solution.py:90
  105.7 1.8 copy-start.3
  105.7 1.9 copy-start.6
  111.9 0.8 copy-start.4
  117.5 365.3 %reduce-scatter.6.cloned.1.call-start = ((), (), s32[]{:S(2)}) async-start(), calls=%async_computation.8 | async-start | bytes 3244032 | tf_op jit(solution)/shard_map/reduce_scatter | solution.py:87
  122.8 3.4 copy-start.5
  128.5 20.2 %all-to-all-start.3 = ((bf16[8,40,2048]{2,1,0:T(8,128)(2,1)}), bf16[8,40,2048]{2,1,0:T(8,128)(2,1)}, u32[]{:S(2)}, u32[]{:S(2)}) async-start(bf16[8,40,2048]{2,1,0:T(8,128)(2,1)} %bitcast.77), calls=%async_computation.3 | async-start | bytes 2621440 | tf_op jit(solution)/shard_map/all_to_all | solution.py:77
Sparse Core Ops, SparseCore 0:
  105.8 125.5 reduce-scatter.9
  236.1 121.3 reduce-scatter.7
  361.6 121.1 reduce-scatter.5
where the time goes:
time: 492 us; the launch traced here: 491 us
  waiting for transfers between devices  366 us (74%)
  matrix products  43.4 us (9%)
  local copies, waits for them, and re-layouts  27.8 us (6%)
  starting transfers between devices  23.7 us (5%)
  between operations  13.9 us (3%)
  blocking collectives  8.51 us (2%)
  other arithmetic  7.59 us (2%)
    reduce_scatter x1, waiting for transfers between devices, shards(): lax.psum_scatter(grad_up[None].astype(jnp.bfloat16), 'dp', scatter_dimens...  124 us
    reduce_scatter x1, waiting for transfers between devices, shards(): lax.psum_scatter(grad_gate[None].astype(jnp.bfloat16), 'dp', scatter_dime...  124 us
    unnamed x4, waiting for transfers between devices  80.1 us
    unnamed x20, local copies, waits for them, and re-layouts  25.2 us
    dot_general x4, matrix products, contract_rows(): lax.dot_general(left, right, (((0,), (0,)), ((), ())), preferred_element_...  17.5 us
    all_to_all x1, waiting for transfers between devices, shards(): lax.all_to_all(pair.reshape(groups, cap, width), 'expert', split_axis=0,...  13.2 us
    all_to_all x1, waiting for transfers between devices, shards(): lax.all_to_all(send_x, 'expert', split_axis=0, concat_axis=0, tiled=True)  12.9 us
    dot_general x3, matrix products, contract_cols(): lax.dot_general(left, right, (((1,), (1,)), ((), ())), preferred_element_...  9.9 us
  transfers between devices with their start and end apart: 7, of which 7 were waited for; matrix products, arithmetic and copies ran while one was open for 8% of the time, Pallas kernels for 0%

commit v1 on v0

--- a/solution.py
+++ b/solution.py
@@ -1,7 +1,14 @@
+import functools
+
 import jax
 import jax.numpy as jnp
 from jax import lax
+from jax.experimental import pallas as pl
+from jax.experimental.pallas import tpu as pltpu
 from jax.sharding import PartitionSpec as P
+
+MESH = pl.DeviceIdType.MESH
+NZ = 8
 
 
 def contract_rows(left, right):
@@ -14,6 +21,125 @@
     return lax.dot_general(
         left, right, (((1,), (1,)), ((), ())), preferred_element_type=jnp.float32
     )
+
+
+def reduce_kernel(g0, g1, g2, o0, o1, o2, sib, ring, xbuf, sib_s, sib_r, ring_s, ring_r, x_s, x_r):
+    dp = lax.axis_index("dp")
+    ex = lax.axis_index("expert")
+    xh, z, c = dp // 16, (dp // 2) % NZ, dp % 2
+    up = (xh * 16 + ((z + 1) % NZ) * 2 + c, ex)
+    down = (xh * 16 + ((z + NZ - 1) % NZ) * 2 + c, ex)
+    sibling = (xh * 16 + z * 2 + (1 - c), ex)
+    across = ((1 - xh) * 16 + z * 2 + c, ex)
+    grads, outs = (g0, g1, g2), (o0, o1, o2)
+
+    barrier = pltpu.get_barrier_semaphore()
+    for peer in (up, down, sibling, across):
+        pl.semaphore_signal(barrier, inc=1, device_id=peer, device_id_type=MESH)
+    pl.semaphore_wait(barrier, 4)
+
+    def chunk(d, s):
+        return (z + 2 * NZ - 1 - s) % NZ if d == 0 else (z + 1 + s) % NZ
+
+    def sib_copy(m, d, s):
+        at = chunk(d, s)
+        return pltpu.make_async_remote_copy(
+            src_ref=grads[m].at[d, at, 1 - c],
+            dst_ref=sib.at[m, d, at],
+            send_sem=sib_s.at[m, d, s],
+            recv_sem=sib_r.at[m, d, s],
+            device_id=sibling,
+            device_id_type=MESH,
+        )
+
+    def ring_copy(m, d, s):
+        return pltpu.make_async_remote_copy(
+            src_ref=ring.at[m, d, s],
+            dst_ref=ring.at[m, d, s + 1],
+            send_sem=ring_s.at[m, d, s],
+            recv_sem=ring_r.at[m, d, s],
+            device_id=up if d == 0 else down,
+            device_id_type=MESH,
+        )
+
+    def x_copy(m):
+        return pltpu.make_async_remote_copy(
+            src_ref=ring.at[m, 1 - xh, NZ - 1],
+            dst_ref=xbuf.at[m],
+            send_sem=x_s.at[m],
+            recv_sem=x_r.at[m],
+            device_id=across,
+            device_id_type=MESH,
+        )
+
+    def own(m, d, at):
+        return grads[m][d, at, c].astype(jnp.float32) + sib[m, d, at].astype(jnp.float32)
+
+    @pl.loop(0, NZ)
+    def _(s):
+        for m in range(3):
+            for d in range(2):
+                sib_copy(m, d, s).start()
+
+    for m in range(3):
+        for d in range(2):
+            sib_copy(m, d, 0).wait()
+            ring[m, d, 0] = own(m, d, chunk(d, 0)).astype(jnp.bfloat16)
+            ring_copy(m, d, 0).start()
+
+    @pl.loop(1, NZ - 1)
+    def _(s):
+        for m in range(3):
+            for d in range(2):
+                sib_copy(m, d, s).wait()
+                ring_copy(m, d, s - 1).wait()
+                ring[m, d, s] = (
+                    ring[m, d, s].astype(jnp.float32) + own(m, d, chunk(d, s))
+                ).astype(jnp.bfloat16)
+                ring_copy(m, d, s).start()
+
+    last = NZ - 1
+    for m in range(3):
+        for d in range(2):
+            sib_copy(m, d, last).wait()
+            ring_copy(m, d, last - 1).wait()
+        ring[m, 1 - xh, last] = (
+            ring[m, 1 - xh, last].astype(jnp.float32) + own(m, 1 - xh, z)
+        ).astype(jnp.bfloat16)
+        x_copy(m).start()
+    for m in range(3):
+        x_copy(m).wait()
+        outs[m][...] = (
+            ring[m, xh, last].astype(jnp.float32)
+            + own(m, xh, z)
+            + xbuf[m].astype(jnp.float32)
+        )
+
+
+def reduce_all(g0, g1, g2):
+    rows, cols = 64, g0.shape[1]
+    parts = tuple(g.reshape(2, NZ, 2, rows, cols) for g in (g0, g1, g2))
+    return pl.pallas_call(
+        reduce_kernel,
+        out_shape=[jax.ShapeDtypeStruct((rows, cols), jnp.float32)] * 3,
+        in_specs=[pl.BlockSpec(memory_space=pltpu.VMEM)] * 3,
+        out_specs=[pl.BlockSpec(memory_space=pltpu.VMEM)] * 3,
+        scratch_shapes=[
+            pltpu.VMEM((3, 2, NZ, rows, cols), jnp.bfloat16),
+            pltpu.VMEM((3, 2, NZ, rows, cols), jnp.bfloat16),
+            pltpu.VMEM((3, rows, cols), jnp.bfloat16),
+            pltpu.SemaphoreType.DMA((3, 2, NZ)),
+            pltpu.SemaphoreType.DMA((3, 2, NZ)),
+            pltpu.SemaphoreType.DMA((3, 2, NZ - 1)),
+            pltpu.SemaphoreType.DMA((3, 2, NZ - 1)),
+            pltpu.SemaphoreType.DMA((3,)),
+            pltpu.SemaphoreType.DMA((3,)),
+        ],
+        compiler_params=pltpu.CompilerParams(
+            collective_id=0, has_side_effects=True, vmem_limit_bytes=48 * 2**20
+        ),
+        name="reduce_grads",
+    )(*parts)
 
 
 def shards(tokens, cotangent, probs, routes, live, slot_map, w_gate, w_up, w_down):
@@ -68,7 +194,7 @@
     expert_out = jnp.dot(hidden, down_w, preferred_element_type=jnp.float32)
     prob_part = jnp.sum(expert_out * rows_dy.astype(jnp.float32), -1).astype(jnp.bfloat16)
     scaled = (weight[:, None] * rows_dy.astype(jnp.float32)).astype(jnp.bfloat16)
-    grad_down = contract_rows(hidden, scaled)
+    grad_down = contract_rows(scaled, hidden)
     hidden_grad = contract_cols(scaled, down_w)
     gate_grad = (hidden_grad * up * sig * (1.0 + gate * (1.0 - sig))).astype(jnp.bfloat16)
     up_grad = (hidden_grad * gate * sig).astype(jnp.bfloat16)
@@ -83,16 +209,10 @@
     )
     grad_gate = contract_rows(rows_x, gate_grad)
     grad_up = contract_rows(rows_x, up_grad)
-    gate_share, up_share, down_share = (
-        lax.psum_scatter(
-            grad_gate[None].astype(jnp.bfloat16), "dp", scatter_dimension=1, tiled=True
-        ).astype(jnp.float32),
-        lax.psum_scatter(
-            grad_up[None].astype(jnp.bfloat16), "dp", scatter_dimension=1, tiled=True
-        ).astype(jnp.float32),
-        lax.psum_scatter(
-            grad_down[None].astype(jnp.bfloat16), "dp", scatter_dimension=2, tiled=True
-        ).astype(jnp.float32),
+    down_share, gate_share, up_share = reduce_all(
+        grad_down.astype(jnp.bfloat16),
+        grad_gate.astype(jnp.bfloat16),
+        grad_up.astype(jnp.bfloat16),
     )
     input_grad = contract_rows(by_token, back.reshape(slots, width)).astype(jnp.bfloat16)
     prob_grad = (
@@ -100,7 +220,7 @@
         .reshape(rows, top)
         .astype(jnp.bfloat16)
     )
-    return (input_grad, prob_grad, gate_share, up_share, down_share)
+    return (input_grad, prob_grad, gate_share[None], up_share[None], down_share.T[None])
 
 
 def solution(mesh):

time: 492 us -> 174 us (0.35)
  waiting for transfers between devices: 366 us -> 28.1 us
  Pallas kernels: 0 us -> 63.7 us
  local copies, waits for them, and re-layouts: 27.8 us -> 8.54 us
  between operations: 13.9 us -> 0.84 us
  blocking collectives: 8.51 us -> 0 us
  starting transfers between devices: 23.7 us -> 28.7 us
    reduce_scatter x2 -> x0, waiting for transfers between devices: 248 us -> none  [the longest x1 124 us: shards(): lax.psum_scatter(grad_up[None].astype(jnp.bfloat16), 'dp', scatter_dimens...]
    unnamed x4 -> x0, waiting for transfers between devices: 80.1 us -> none
    pallas_call x0 -> x1, Pallas kernels: none -> 63.7 us  [reduce_all(): pl.pallas_call(reduce_kernel, out_shape=[jax.ShapeDtypeStruct((rows, cols...]
    unnamed x20 -> x28, local copies, waits for them, and re-layouts: 25.2 us -> 5.39 us
    all_to_all x1, waiting for transfers between devices: 13.2 us -> 0.01 us  [shards(): lax.all_to_all(pair.reshape(groups, cap, width), 'expert', split_axis=0,...]
    all_to_all x1 -> x0, blocking collectives: 8.51 us -> none  [shards(): lax.all_to_all(send_p, 'expert', split_axis=0, concat_axis=0, tiled=True)]
    all_to_all x0 -> x1, starting transfers between devices: none -> 5.29 us  [shards(): lax.all_to_all(send_p, 'expert', split_axis=0, concat_axis=0, tiled=True)]
  transfers between devices with their start and end apart: 7 -> 5, of which waited for: 7 -> 4; matrix products, arithmetic and copies ran while one was open for 8% -> 14% of each run, Pallas kernels for 0% -> 37%
where the time goes in v1:
time: 174 us; the launch traced here: 173 us
  Pallas kernels  63.7 us (37%)
  matrix products  39 us (22%)
  starting transfers between devices  28.7 us (16%)
  waiting for transfers between devices  28.1 us (16%)
  local copies, waits for them, and re-layouts  8.54 us (5%)
  other arithmetic  4.43 us (3%)
    pallas_call x1, Pallas kernels, reduce_all(): pl.pallas_call(reduce_kernel, out_shape=[jax.ShapeDtypeStruct((rows, cols...  63.7 us
    dot_general x4, matrix products, contract_rows(): lax.dot_general(left, right, (((0,), (0,)), ((), ())), preferred_element_...  15.8 us
    all_to_all x1, waiting for transfers between devices, shards(): lax.all_to_all(send_x, 'expert', split_axis=0, concat_axis=0, tiled=True)  12.9 us
    all_to_all x1, waiting for transfers between devices, shards(): lax.all_to_all(send_dy, 'expert', split_axis=0, concat_axis=0, tiled=True)  8.17 us
    dot_general x3, matrix products, contract_cols(): lax.dot_general(left, right, (((1,), (1,)), ((), ())), preferred_element_...  7.13 us
    all_to_all x1, starting transfers between devices, shards(): lax.all_to_all(pair.reshape(groups, cap, width), 'expert', split_axis=0,...  6.24 us
    all_to_all x1, starting transfers between devices, shards(): lax.all_to_all(send_x, 'expert', split_axis=0, concat_axis=0, tiled=True)  6.11 us
    all_to_all x1, starting transfers between devices, shards(): lax.all_to_all(send_dy, 'expert', split_axis=0, concat_axis=0, tiled=True)  5.88 us
  transfers between devices with their start and end apart: 5, of which 4 were waited for; matrix products, arithmetic and copies ran while one was open for 14% of the time, Pallas kernels for 37%

profile of v1, /device:TPU:24, one launch (start us, length us, event | category | flops | bytes accessed | tf_op | source)
XLA Modules:
  0.0 173.3 jit_solution(4935160837054049441)
XLA Ops:
  0.6 0.0 copy-start
  0.6 0.9 select_reduce_fusion.2
  1.6 0.1 copy.27
  1.7 0.1 eq.92
  1.8 0.1 eq.97
  2.0 0.7 broadcast_compare_fusion
  2.6 0.1 broadcast_in_dim.43
  2.7 0.1 eq.88
  2.8 0.1 broadcast_in_dim.44.clone
  2.9 0.1 eq.96
  3.0 0.1 fusion.29
  3.1 0.6 reduce-window.6
  3.7 0.2 slice_reduce_fusion
  3.9 0.1 fusion.26
  4.0 0.1 reduce_sum.58
  4.2 0.1 copy.30
  4.3 0.1 convert_reduce_fusion
  4.3 0.0 copy-start.2
  4.3 2.6 %convolution_convert_fusion.3 = bf16[320,2048]{1,0:T(8,128)(2,1)} fusion(bf16[128,2048]{1,0:T(8,128)(2,1)} %param.9, bf16[320,128]{1,0:T(8,128)(2,1)S(1)} %convert_reduce_fusion), kind=kOutput, calls=%fused_computation.17 | convolution fusion | flops 168427520 | bytes 1916928 | tf_op jit(solution)/shard_map/dot_general | solution.py:165
  7.0 6.1 %all-to-all-start.2 = ((bf16[8,40,2048]{2,1,0:T(8,128)(2,1)}), bf16[8,40,2048]{2,1,0:T(8,128)(2,1)}, u32[]{:S(2)}, u32[]{:S(2)}) async-start(bf16[8,40,2048]{2,1,0:T(8,128)(2,1)} %bitcast.74), calls=%async_computation.2 | async-start | bytes 2621440 | tf_op jit(solution)/shard_map/all_to_all | solution.py:183
  13.1 2.6 %convolution_convert_fusion.4 = bf16[320,2048]{1,0:T(8,128)(2,1)} fusion(bf16[128,2048]{1,0:T(8,128)(2,1)} %param.10, bf16[320,128]{1,0:T(8,128)(2,1)S(1)} %convert_reduce_fusion), kind=kOutput, calls=%fused_computation.18 | convolution fusion | flops 168427520 | bytes 1916928 | tf_op jit(solution)/shard_map/dot_general | solution.py:170
  15.7 0.0 copy-done.2
  15.7 12.9 %all-to-all-done.2 = bf16[8,40,2048]{2,1,0:T(8,128)(2,1)} async-done(((bf16[8,40,2048]{2,1,0:T(8,128)(2,1)}), bf16[8,40,2048]{2,1,0:T(8,128)(2,1)}, u32[]{:S(2)}, u32[]{:S(2)}) %all-to-all-start.2) | async-done | bytes 1310752 | tf_op jit(solution)/shard_map/all_to_all | solution.py:183
  28.6 5.9 %all-to-all-start.1 = ((bf16[8,40,2048]{2,1,0:T(8,128)(2,1)}), bf16[8,40,2048]{2,1,0:T(8,128)(2,1)}, u32[]{:S(2)}, u32[]{:S(2)}) async-start(bf16[8,40,2048]{2,1,0:T(8,128)(2,1)} %bitcast.73), calls=%async_computation.1 | async-start | bytes 2621440 | tf_op jit(solution)/shard_map/all_to_all | solution.py:189
  34.5 3.5 %fusion.2 = f32[320,768]{1,0:T(8,128)S(1)} fusion(bf16[320,2048]{1,0:T(8,128)(2,1)} %bitcast.7, bf16[1,2048,768]{2,1,0:T(8,128)(2,1)} %param.15), kind=kOutput, calls=%fused_computation.5 | convolution fusion | flops 1006632960 | bytes 5439488 | tf_op jit(solution)/shard_map/dot_general | solution.py:187
  37.9 0.0 copy-start.7
  38.0 1.0 copy-done.7
  38.9 0.0 copy-done
  38.9 3.6 %multiply_convert_fusion.3 = (bf16[320,768]{1,0:T(8,128)(2,1)}, f32[320,768]{1,0:T(8,128)}) fusion(f32[320,768]{1,0:T(8,128)S(1)} %fusion.2, bf16[320,2048]{1,0:T(8,128)(2,1)} %bitcast.7, bf16[1,2048,768]{2,1,0:T(8,128)(2,1)S(1)} %copy-done), kind=kOutput, calls=%fused_computation.25 | convolution fusion | flops 1008107520 | bytes 6914048 | tf_op jit(solution)/shard_map/dot_general | solution.py:188
  42.5 8.2 %all-to-all-done.1 = bf16[8,40,2048]{2,1,0:T(8,128)(2,1)} async-done(((bf16[8,40,2048]{2,1,0:T(8,128)(2,1)}), bf16[8,40,2048]{2,1,0:T(8,128)(2,1)}, u32[]{:S(2)}, u32[]{:S(2)}) %all-to-all-start.1) | async-done | bytes 1310752 | tf_op jit(solution)/shard_map/all_to_all | solution.py:189
  50.7 3.7 %fusion.21 = bf16[320]{0:T(512)(128)(2,1)S(1)} fusion(bf16[320,768]{1,0:T(8,128)(2,1)} %get-tuple-element.35, bf16[1,768,2048]{2,1,0:T(8,128)(2,1)} %param.17, bf16[320,2048]{1,0:T(8,128)(2,1)} %bitcast.47), kind=kOutput, calls=%fused_computation.23 | convolution fusion | flops 1008598720 | bytes 4948608 | tf_op jit(solution)/shard_map/dot_general | solution.py:194
  54.4 0.7 convert_element_type.172
  55.1 5.2 %all-to-all-start.4 = ((bf16[8,1,40]{2,1,0:T(2,128)(2,1)}), bf16[8,1,40]{2,1,0:T(2,128)(2,1)S(1)}, u32[]{:S(2)}, u32[]{:S(2)}) async-start(bf16[8,1,40]{2,1,0:T(2,128)(2,1)} %convert_element_type.172), calls=%async_computation.4 | async-start | bytes 8192 | tf_op jit(solution)/shard_map/all_to_all | solution.py:206
  60.3 0.0 copy-done.3
  60.3 0.1 copy.31
  60.4 0.1 reshape.179
  60.6 3.7 %all-to-all-done.4 = bf16[8,1,40]{2,1,0:T(2,128)(2,1)S(1)} async-done(((bf16[8,1,40]{2,1,0:T(2,128)(2,1)}), bf16[8,1,40]{2,1,0:T(2,128)(2,1)S(1)}, u32[]{:S(2)}, u32[]{:S(2)}) %all-to-all-start.4) | async-done | bytes 672 | tf_op jit(solution)/shard_map/all_to_all | solution.py:206
  64.4 0.1 reshape.182
  64.4 0.2 select_reduce_fusion
  64.7 0.7 convert_element_type.171
  65.3 5.3 %all-to-all-start = ((bf16[8,1,40]{2,1,0:T(2,128)(2,1)}), bf16[8,1,40]{2,1,0:T(2,128)(2,1)S(1)}, u32[]{:S(2)}, u32[]{:S(2)}) async-start(bf16[8,1,40]{2,1,0:T(2,128)(2,1)} %convert_element_type.171), calls=%async_computation | async-start | bytes 8192 | tf_op jit(solution)/shard_map/all_to_all | solution.py:184
  70.6 0.2 convert_element_type.159
  70.8 0.6 copy.34
  71.4 3.3 %all-to-all-done = bf16[8,1,40]{2,1,0:T(2,128)(2,1)S(1)} async-done(((bf16[8,1,40]{2,1,0:T(2,128)(2,1)}), bf16[8,1,40]{2,1,0:T(2,128)(2,1)S(1)}, u32[]{:S(2)}, u32[]{:S(2)}) %all-to-all-start) | async-done | bytes 672 | tf_op jit(solution)/shard_map/all_to_all | solution.py:184
  74.7 1.7 multiply_convert_fusion.1
  76.4 0.0 copy-done.8
  76.4 0.1 copy-done.11
  76.6 3.6 %multiply_convert_fusion.4 = (bf16[320,768]{1,0:T(8,128)(2,1)S(1)}, bf16[320,768]{1,0:T(8,128)(2,1)S(1)}) fusion(f32[320,768]{1,0:T(8,128)S(1)} %copy-done.8, f32[320,768]{1,0:T(8,128)S(1)} %copy-done.11, bf16[320,2048]{1,0:T(8,128)(2,1)S(1)} %bitcast.78, bf16[1,768,2048]{2,1,0:T(8,128)(2,1)} %param.17), kind=kOutput, calls=%fused_computation.26 | convolution fusion | flops 1009827840 | bytes 7405568 | tf_op jit(solution)/shard_map/dot_general | solution.py:21
  80.2 1.2 fusion
  81.5 2.3 %fusion.18 = bf16[320,2048]{1,0:T(8,128)(2,1)} fusion(f32[320,2048]{1,0:T(8,128)S(1)} %fusion, bf16[320,768]{1,0:T(8,128)(2,1)S(1)} %get-tuple-element.33, bf16[1,2048,768]{2,1,0:T(8,128)(2,1)S(1)} %copy-done), kind=kOutput, calls=%fused_computation.19 | convolution fusion | flops 1007943680 | bytes 7569408 | tf_op jit(solution)/shard_map/dot_general | solution.py:21
  83.8 6.2 %all-to-all-start.3 = ((bf16[8,40,2048]{2,1,0:T(8,128)(2,1)}), bf16[8,40,2048]{2,1,0:T(8,128)(2,1)}, u32[]{:S(2)}, u32[]{:S(2)}) async-start(bf16[8,40,2048]{2,1,0:T(8,128)(2,1)} %bitcast.77), calls=%async_computation.3 | async-start | bytes 2621440 | tf_op jit(solution)/shard_map/all_to_all | solution.py:203
  90.0 0.1 reshape.183
  90.1 5.0 %convolution_convert_fusion = bf16[2048,768]{1,0:T(8,128)(2,1)} fusion(bf16[320,2048]{1,0:T(8,128)(2,1)} %bitcast.7, bf16[320,768]{1,0:T(8,128)(2,1)} %copy-done.9), kind=kOutput, calls=%fused_computation | convolution fusion | flops 1008205824 | bytes 4947968 | tf_op jit(solution)/shard_map/dot_general | solution.py:15
  95.1 0.0 copy-done.6
  95.1 4.9 %convolution_convert_fusion.1 = bf16[2048,768]{1,0:T(8,128)(2,1)} fusion(bf16[320,2048]{1,0:T(8,128)(2,1)} %bitcast.7, bf16[320,768]{1,0:T(8,128)(2,1)S(1)} %copy-done.6), kind=kOutput, calls=%fused_computation.1 | convolution fusion | flops 1008205824 | bytes 4947968 | tf_op jit(solution)/shard_map/dot_general | solution.py:15
  100.0 3.3 %convolution_convert_fusion.2 = bf16[2048,768]{1,0:T(8,128)(2,1)S(1)} fusion(bf16[320,768]{1,0:T(8,128)(2,1)S(1)} %copy-done.10, f32[320]{0:T(512)S(1)} %reshape.183, bf16[320,2048]{1,0:T(8,128)(2,1)} %bitcast.47), kind=kOutput, calls=%fused_computation.2 | convolution fusion | flops 1010171904 | bytes 4949248 | tf_op jit(solution)/shard_map/dot_general | solution.py:15
  103.3 63.7 %reduce_grads.1 = (f32[64,768]{1,0:T(8,128)S(1)}, f32[64,768]{1,0:T(8,128)S(1)}, f32[64,768]{1,0:T(8,128)S(1)}) custom-call(bf16[2,8,2,64,768]{4,3,2,1,0:T(8,128)(2,1)S(1)} %bitcast.69, bf16[2,8,2,64,768]{4,3,2,1,0:T(8,128)(2,1)} %bitcast.76, bf16[2,8,2,64,768]{4,3,2,1,0:T(8,128)(2,1)} %bitcast.75), custom_call_target="tpu_custom_call" | custom-call | tf_op jit(solution)/shard_map/reduce_grads/pallas_call | solution.py:122
  167.0 0.0 copy-start.1
  167.0 0.7 copy-done.1
  167.7 0.0 all-to-all-done.3
  167.7 2.6 %convolution_convert_fusion.5 = bf16[128,2048]{1,0:T(8,128)(2,1)} fusion(bf16[320,2048]{1,0:T(8,128)(2,1)} %bitcast.11, bf16[320,128]{1,0:T(8,128)(2,1)} %copy-done.2), kind=kOutput, calls=%fused_computation.22 | convolution fusion | flops 168034304 | bytes 1916928 | tf_op jit(solution)/shard_map/dot_general | solution.py:15
  170.3 1.6 copy.38
  171.9 0.7 copy.39
  172.6 0.7 copy.40
  (19 shorter events, 0.1 us)
Async XLA Ops:
  0.6 38.3 %copy-start = (bf16[1,2048,768]{2,1,0:T(8,128)(2,1)S(1)}, bf16[1,2048,768]{2,1,0:T(8,128)(2,1)}, u32[]{:S(2)}) copy-start(bf16[1,2048,768]{2,1,0:T(8,128)(2,1)} %param.16) | copy-start | bytes 9437188
  4.3 11.4 %copy-start.2 = (bf16[320,128]{1,0:T(8,128)(2,1)}, bf16[320,128]{1,0:T(8,128)(2,1)S(1)}, u32[]{:S(2)}) copy-start(bf16[320,128]{1,0:T(8,128)(2,1)S(1)} %convert_reduce_fusion) | copy-start | bytes 245764
  7.0 21.6 %all-to-all-start.2 = ((bf16[8,40,2048]{2,1,0:T(8,128)(2,1)}), bf16[8,40,2048]{2,1,0:T(8,128)(2,1)}, u32[]{:S(2)}, u32[]{:S(2)}) async-start(bf16[8,40,2048]{2,1,0:T(8,128)(2,1)} %bitcast.74), calls=%async_computation.2 | async-start | bytes 2621440 | tf_op jit(solution)/shard_map/all_to_all | solution.py:183
  28.6 22.1 %all-to-all-start.1 = ((bf16[8,40,2048]{2,1,0:T(8,128)(2,1)}), bf16[8,40,2048]{2,1,0:T(8,128)(2,1)}, u32[]{:S(2)}, u32[]{:S(2)}) async-start(bf16[8,40,2048]{2,1,0:T(8,128)(2,1)} %bitcast.73), calls=%async_computation.1 | async-start | bytes 2621440 | tf_op jit(solution)/shard_map/all_to_all | solution.py:189
  37.9 1.0 copy-start.7
  50.7 9.6 %copy-start.3 = (bf16[128,2]{0,1:T(2,128)(2,1)S(1)}, bf16[128,2]{0,1:T(2,128)(2,1)}, u32[]{:S(2)}) copy-start(bf16[128,2]{0,1:T(2,128)(2,1)} %param.11) | copy-start | bytes 1540
  55.1 9.2 %all-to-all-start.4 = ((bf16[8,1,40]{2,1,0:T(2,128)(2,1)}), bf16[8,1,40]{2,1,0:T(2,128)(2,1)S(1)}, u32[]{:S(2)}, u32[]{:S(2)}) async-start(bf16[8,1,40]{2,1,0:T(2,128)(2,1)} %convert_element_type.172), calls=%async_computation.4 | async-start | bytes 8192 | tf_op jit(solution)/shard_map/all_to_all | solution.py:206
  65.3 9.3 %all-to-all-start = ((bf16[8,1,40]{2,1,0:T(2,128)(2,1)}), bf16[8,1,40]{2,1,0:T(2,128)(2,1)S(1)}, u32[]{:S(2)}, u32[]{:S(2)}) async-start(bf16[8,1,40]{2,1,0:T(2,128)(2,1)} %convert_element_type.171), calls=%async_computation | async-start | bytes 8192 | tf_op jit(solution)/shard_map/all_to_all | solution.py:184
  74.7 1.8 %copy-start.8 = (f32[320,768]{1,0:T(8,128)S(1)}, f32[320,768]{1,0:T(8,128)}, u32[]{:S(2)}) copy-start(f32[320,768]{1,0:T(8,128)} %copy-done.7) | copy-start | bytes 2949124
  74.7 1.9 %copy-start.11 = (f32[320,768]{1,0:T(8,128)S(1)}, f32[320,768]{1,0:T(8,128)}, u32[]{:S(2)}) copy-start(f32[320,768]{1,0:T(8,128)} %get-tuple-element.36) | copy-start | bytes 2949124
  76.6 3.6 %copy-start.4 = (bf16[1,2048,768]{2,1,0:T(8,128)(2,1)S(1)}, bf16[1,2048,768]{2,1,0:T(8,128)(2,1)}, u32[]{:S(2)}) copy-start(bf16[1,2048,768]{2,1,0:T(8,128)(2,1)} %param.15) | copy-start | bytes 9437188
  80.2 1.2 copy-start.5
  80.2 1.2 copy-start.9
  83.8 83.9 %all-to-all-start.3 = ((bf16[8,40,2048]{2,1,0:T(8,128)(2,1)}), bf16[8,40,2048]{2,1,0:T(8,128)(2,1)}, u32[]{:S(2)}, u32[]{:S(2)}) async-start(bf16[8,40,2048]{2,1,0:T(8,128)(2,1)} %bitcast.77), calls=%async_computation.3 | async-start | bytes 2621440 | tf_op jit(solution)/shard_map/all_to_all | solution.py:203
  90.1 5.0 %copy-start.6 = (bf16[320,768]{1,0:T(8,128)(2,1)S(1)}, bf16[320,768]{1,0:T(8,128)(2,1)}, u32[]{:S(2)}) copy-start(bf16[320,768]{1,0:T(8,128)(2,1)} %copy-done.5) | copy-start | bytes 1474564
  95.1 4.9 %copy-start.10 = (bf16[320,768]{1,0:T(8,128)(2,1)S(1)}, bf16[320,768]{1,0:T(8,128)(2,1)}, u32[]{:S(2)}) copy-start(bf16[320,768]{1,0:T(8,128)(2,1)} %get-tuple-element.35) | copy-start | bytes 1474564
  167.0 0.7 copy-start.1

commit v2 on v0

v2 whole, which is shorter than its diff:
```python
import jax
import jax.numpy as jnp
from jax import lax
from jax.experimental import pallas as pl
from jax.experimental.pallas import tpu as pltpu
from jax.sharding import PartitionSpec as P

MESH = pl.DeviceIdType.MESH
F32, BF16 = jnp.float32, jnp.bfloat16
NZ = 8
NE = 8
TOK = 128
WIDE = 2048
HALF = 1024
FF = 768
MAIN = 32
REST = 8
ROWS = NE * (MAIN + REST)
LAST = NZ - 1


def mm(a, b):
    return jnp.dot(a, b, preferred_element_type=F32)


def mm_tn(a, b):
    return lax.dot_general(a, b, (((0,), (0,)), ((), ())), preferred_element_type=F32)


def mm_nt(a, b):
    return lax.dot_general(a, b, (((1,), (1,)), ((), ())), preferred_element_type=F32)


def cols_at(start, size):
    return pl.ds(pl.multiple_of(start, size), size)


def one_hot(hit):
    return jnp.where(hit, 1.0, 0.0).astype(BF16)


def layer_kernel(
    slot_ref, live_ref, routes_ref, probs_ref, tok_ref, cot_ref, wg_hbm, wu_hbm, wd_hbm,
    in_ref, pg_ref, o_down, o_gate, o_up,
    wg, wu, wd, w_sem,
    pick, pick_a, pick_b, pick48,
    sx, sxt, sdy, sdyt, sp, x, xt, dy, dyt, prob,
    hid, phid, act1, act2, gg, ug, pp,
    pair, pairt, sbp, back, backt, bp,
    grads, sib, ring, xbuf,
    a2a_s, a2a_r, sib_s, sib_r, ring_s, ring_r, x_s, x_r,
):
    dp = lax.axis_index("dp")
    me = lax.axis_index("expert")
    xh, z, c = dp // 16, (dp // 2) % NZ, dp % 2
    up = (xh * 16 + ((z + 1) % NZ) * 2 + c, me)
    down = (xh * 16 + ((z + NZ - 1) % NZ) * 2 + c, me)
    sibling = (xh * 16 + z * 2 + (1 - c), me)
    across = ((1 - xh) * 16 + z * 2 + c, me)

    weights = [
        pltpu.make_async_copy(src, dst, w_sem.at[i])
        for i, (src, dst) in enumerate(((wg_hbm, wg), (wu_hbm, wu), (wd_hbm, wd)))
    ]
    for w in weights:
        w.start()

    barrier = pltpu.get_barrier_semaphore()
    for peer in (up, down, sibling, across):
        pl.semaphore_signal(barrier, inc=1, device_id=peer, device_id_type=MESH)
    for k in range(1, NE):
        pl.semaphore_signal(
            barrier, inc=1, device_id=(dp, (me + k) % NE), device_id_type=MESH
        )

    slot_iota = lax.broadcasted_iota(jnp.int32, (NE, TOK), 0)
    lane = lax.broadcasted_iota(jnp.int32, (1, TOK), 1)
    alive = jnp.where(lane < TOK // 2, live_ref[0], live_ref[1]) == 1
    owners = []
    for k in range(2):
        r = routes_ref[k : k + 1, :]
        o = jnp.zeros((1, TOK), jnp.int32)
        for e in range(NE):
            o = jnp.where(r == e, slot_ref[e], o)
        owners.append(jnp.where(alive, o, -1))
    taken = sum(jnp.where(slot_iota == o, 1.0, 0.0) for o in owners).astype(BF16)
    earlier = lax.broadcasted_iota(jnp.int32, (TOK, TOK), 0) < lax.broadcasted_iota(
        jnp.int32, (TOK, TOK), 1
    )
    before = mm(taken, one_hot(earlier))
    mains, rests, alls = [], [], []
    for o in owners:
        pos = jnp.sum(jnp.where(slot_iota == o, before, 0.0), 0, keepdims=True).astype(jnp.int32)
        mains.append(jnp.where((o >= 0) & (pos < MAIN), o * MAIN + pos, -1))
        rests.append(jnp.where((o >= 0) & (pos >= MAIN), o * 2 * REST + pos - MAIN, -1))
        alls.append(jnp.where(o >= 0, o * 48 + pos, -1))
    row = lax.broadcasted_iota(jnp.int32, (NE * MAIN, TOK), 0)
    pick[...] = one_hot((row == mains[0]) | (row == mains[1]))
    row = lax.broadcasted_iota(jnp.int32, (NE * 2 * REST, TOK), 0)
    pick_a[...] = one_hot((row == rests[0]) | (row == rests[1]))
    low = row - REST
    pick_b[...] = one_hot(
        ((low == rests[0]) & (rests[0] >= 0)) | ((low == rests[1]) & (rests[1] >= 0))
    )

    def dispatch(src, main, rest):
        @pl.loop(0, 4)
        def _(n):
            cols = cols_at(n * 512, 512)
            main[:, cols] = mm(pick[...], src[:, cols]).astype(BF16)

        @pl.loop(0, 2)
        def _(n):
            cols = cols_at(n * 512, 512)
            more = cols_at(HALF + n * 512, 512)
            rest[:, cols] = (
                mm(pick_a[...], src[:, cols]) + mm(pick_b[...], src[:, more])
            ).astype(BF16)

    def piece(ref, kind, e):
        if kind % 3 == 0:
            return ref.at[pl.ds(pl.multiple_of(e * MAIN, MAIN), MAIN)]
        if kind % 3 == 1:
            return ref.at[pl.ds(pl.multiple_of(e * 2 * REST, 2 * REST), 2 * REST)]
        return ref.at[e]

    exchanged = (
        (sx, x), (sxt, xt), (sp, prob),
        (sdy, dy), (sdyt, dyt), None,
        (pair, back), (pairt, backt), (sbp, bp),
    )

    def exchange(kind, k):
        src, dst = exchanged[kind]
        to = (me + k) % NE
        return pltpu.make_async_remote_copy(
            src_ref=piece(src, kind, to),
            dst_ref=piece(dst, kind, me),
            send_sem=a2a_s.at[kind, k],
            recv_sem=a2a_r.at[kind, k],
            device_id=(dp, to),
            device_id_type=MESH,
        )

    def start_all(kinds):
        @pl.loop(1, NE)
        def _(k):
            for kind in kinds:
                exchange(kind, k).start()

    def keep_own(kinds):
        for kind in kinds:
            src, dst = exchanged[kind]
            if kind % 3 == 2:
                dst[me] = src[me]
            else:
                size = MAIN if kind % 3 == 0 else 2 * REST
                rows = pl.ds(pl.multiple_of(me * size, size), size)
                dst[rows, :] = src[rows, :]

    def wait_sent(kinds):
        @pl.loop(1, NE)
        def _(k):
            for kind in kinds:
                exchange(kind, k).wait_send()

    def wait_got(kinds):
        @pl.loop(1, NE)
        def _(k):
            for kind in kinds:
                exchange(kind, k).wait_recv()

    dispatch(tok_ref, sx, sxt)
    pl.semaphore_wait(barrier, 4 + NE - 1)
    start_all((0, 1))
    row = lax.broadcasted_iota(jnp.int32, (NE * 48, TOK), 0)
    total = jnp.zeros((NE * 48, 1), F32)
    for k in range(2):
        hit = jnp.where(row == alls[k], 1.0, 0.0)
        pick48[k] = hit
        total += jnp.sum(hit * probs_ref[k : k + 1, :], 1, keepdims=True)
    sp[...] = jnp.broadcast_to(total, (NE * 48, 128)).astype(BF16).reshape(NE, 48, 128)
    keep_own((0, 1, 2))
    dispatch(cot_ref, sdy, sdyt)
    keep_own((3, 4))
    wait_sent((0, 1))
    start_all((3, 4, 2))

    part = lax.broadcasted_iota(jnp.int32, (NE * REST, NE * 2 * REST), 0)
    from_row = lax.broadcasted_iota(jnp.int32, (NE * REST, NE * 2 * REST), 1)
    first = (part // REST) * 2 * REST + part % REST
    take_a, take_b = one_hot(from_row == first), one_hot(from_row == first + REST)

    def join(main, rest):
        rows = pl.ds(NE * MAIN, NE * REST)

        @pl.loop(0, 2)
        def _(n):
            cols = cols_at(n * 512, 512)
            half = rest[:, cols]
            main[rows, cols] = mm(take_a, half).astype(BF16)
            main[rows, cols_at(HALF + n * 512, 512)] = mm(take_b, half).astype(BF16)

    wait_got((0, 1))
    join(x, xt)
    weights[0].wait()
    weights[1].wait()

    @pl.loop(0, FF // 256)
    def _(n):
        cols = cols_at(n * 256, 256)
        gate = mm(x[...], wg[:, cols])
        u = mm(x[...], wu[:, cols])
        sig = jax.nn.sigmoid(gate)
        gs = gate * sig
        hid[:, cols] = (gs * u).astype(BF16)
        act1[:, cols] = u * sig * (1.0 + gate * (1.0 - sig))
        act2[:, cols] = gs

    weights[2].wait()
    wait_got((2,))
    p_all = prob[...].astype(F32)
    weight = jnp.concatenate(
        [
            p_all[:, :MAIN].reshape(NE * MAIN, 128),
            p_all[:, MAIN : MAIN + REST].reshape(NE * REST, 128),
        ],
        0,
    )[:, :1]
    phid[...] = (weight * hid[...].astype(F32)).astype(BF16)
    wait_got((3, 4))
    join(dy, dyt)

    def chunk(d, s):
        return (z + 2 * NZ - 1 - s) % NZ if d == 0 else (z + 1 + s) % NZ

    def sib_copy(m, d, s):
        at = chunk(d, s)
        return pltpu.make_async_remote_copy(
            src_ref=grads.at[m, d, at, 1 - c],
            dst_ref=sib.at[m, d, at],
            send_sem=sib_s.at[m, d, s],
            recv_sem=sib_r.at[m, d, s],
            device_id=sibling,
            device_id_type=MESH,
        )

    def ring_copy(m, d, s):
        return pltpu.make_async_remote_copy(
            src_ref=ring.at[m, d, s],
            dst_ref=ring.at[m, d, s + 1],
            send_sem=ring_s.at[m, d, s],
            recv_sem=ring_r.at[m, d, s],
            device_id=up if d == 0 else down,
            device_id_type=MESH,
        )

    def x_copy(m):
        return pltpu.make_async_remote_copy(
            src_ref=ring.at[m, 1 - xh, LAST],
            dst_ref=xbuf.at[m],
            send_sem=x_s.at[m],
            recv_sem=x_r.at[m],
            device_id=across,
            device_id_type=MESH,
        )

    def own(m, d, at):
        return grads[m, d, at, c].astype(F32) + sib[m, d, at].astype(F32)

    def make_grads(left, rights):
        @pl.loop(0, NZ)
        def _(s):
            lhs = jnp.concatenate(
                [
                    left[:, cols_at(chunk(0, s) * 128, 128)],
                    left[:, cols_at(HALF + chunk(1, s) * 128, 128)],
                ],
                1,
            )
            for m, right in rights:
                out = mm_tn(lhs, right[...]).astype(BF16)
                for d in range(2):
                    grads[m, d, chunk(d, s)] = out[d * 128 : d * 128 + 128].reshape(2, 64, FF)
                    sib_copy(m, d, s).start()

    def ring_start(m):
        for d in range(2):
            sib_copy(m, d, 0).wait()
            ring[m, d, 0] = own(m, d, chunk(d, 0)).astype(BF16)
            ring_copy(m, d, 0).start()

    def ring_step(m, s):
        for d in range(2):
            sib_copy(m, d, s).wait()
            ring_copy(m, d, s - 1).wait()
            ring[m, d, s] = (ring[m, d, s].astype(F32) + own(m, d, chunk(d, s))).astype(BF16)
            ring_copy(m, d, s).start()

    def ring_end(m):
        for d in range(2):
            sib_copy(m, d, LAST).wait()
            ring_copy(m, d, LAST - 1).wait()
        ring[m, 1 - xh, LAST] = (
            ring[m, 1 - xh, LAST].astype(F32) + own(m, 1 - xh, z)
        ).astype(BF16)
        x_copy(m).start()

    make_grads(dy, ((0, phid),))
    ring_start(0)

    pp[...] = jnp.zeros_like(pp)

    @pl.loop(0, FF // 256)
    def _(n):
        cols = cols_at(n * 256, 256)
        dyw = mm_nt(dy[...], wd[cols, :])
        pp[...] += jnp.sum(hid[:, cols].astype(F32) * dyw, 1, keepdims=True)
        hg = dyw * weight
        gg[:, cols] = (hg * act1[:, cols]).astype(BF16)
        ug[:, cols] = (hg * act2[:, cols]).astype(BF16)

    ring_step(0, 1)
    make_grads(x, ((1, gg), (2, ug)))
    ring_start(1)
    ring_start(2)
    ring_step(0, 2)

    @pl.loop(0, WIDE // 256)
    def _(n):
        cols = cols_at(n * 256, 256)
        pair[:, cols] = (mm_nt(gg[...], wg[cols, :]) + mm_nt(ug[...], wu[cols, :])).astype(BF16)

    rows = pl.ds(NE * MAIN, NE * REST)

    @pl.loop(0, 2)
    def _(n):
        cols = cols_at(n * 512, 512)
        pairt[:, cols] = (
            mm_tn(take_a, pair[rows, cols])
            + mm_tn(take_b, pair[rows, cols_at(HALF + n * 512, 512)])
        ).astype(BF16)

    part = jnp.broadcast_to(pp[...], (ROWS, 128))
    sbp[:, :MAIN] = part[: NE * MAIN].reshape(NE, MAIN, 128).astype(BF16)
    sbp[:, MAIN:] = jnp.concatenate(
        [part[NE * MAIN :].reshape(NE, REST, 128), jnp.zeros((NE, REST, 128), F32)], 1
    ).astype(BF16)
    start_all((6, 7, 8))
    keep_own((6, 7, 8))

    @pl.loop(1, 5)
    def _(s):
        ring_step(1, s)
        ring_step(2, s)
        ring_step(0, s + 2)

    ring_step(1, 5)
    ring_step(2, 5)
    ring_end(0)
    ring_step(1, 6)
    ring_step(2, 6)

    wait_got((6, 7, 8))

    @pl.loop(0, 2)
    def _(n):
        cols = cols_at(n * 512, 512)
        more = cols_at(HALF + n * 512, 512)
        in_ref[:, cols] = (
            mm_tn(pick[...], back[:, cols]) + mm_tn(pick_a[...], backt[:, cols])
        ).astype(BF16)
        in_ref[:, more] = (
            mm_tn(pick[...], back[:, more]) + mm_tn(pick_b[...], backt[:, cols])
        ).astype(BF16)

    parts = bp[...].astype(F32).reshape(NE * 48, 128)
    for k in range(2):
        pg_ref[k : k + 1, :] = jnp.sum(pick48[k] * parts, 0, keepdims=True)

    ring_end(1)
    ring_end(2)
    for m, out in enumerate((o_down, o_gate, o_up)):
        x_copy(m).wait()
        out[...] = ring[m, xh, LAST].astype(F32) + own(m, xh, z) + xbuf[m].astype(F32)
    wait_sent((2, 3, 4, 6, 7, 8))


def layer(slot_map, live, routes, probs, tokens, cotangent, wg, wu, wd):
    vmem, smem = pl.BlockSpec(memory_space=pltpu.VMEM), pl.BlockSpec(memory_space=pltpu.SMEM)
    anywhere = pl.BlockSpec(memory_space=pl.ANY)
    dma = pltpu.SemaphoreType.DMA
    return pl.pallas_call(
        layer_kernel,
        out_shape=[
            jax.ShapeDtypeStruct((TOK, WIDE), BF16),
            jax.ShapeDtypeStruct((2, TOK), F32),
        ]
        + [jax.ShapeDtypeStruct((64, FF), F32)] * 3,
        in_specs=[smem, smem, vmem, vmem, vmem, vmem, anywhere, anywhere, anywhere],
        out_specs=[vmem] * 5,
        scratch_shapes=[
            pltpu.VMEM((WIDE, FF), BF16),
            pltpu.VMEM((WIDE, FF), BF16),
            pltpu.VMEM((FF, WIDE), BF16),
            dma((3,)),
            pltpu.VMEM((NE * MAIN, TOK), BF16),
            pltpu.VMEM((NE * 2 * REST, TOK), BF16),
            pltpu.VMEM((NE * 2 * REST, TOK), BF16),
            pltpu.VMEM((2, NE * 48, TOK), F32),
            pltpu.VMEM((NE * MAIN, WIDE), BF16),
            pltpu.VMEM((NE * 2 * REST, HALF), BF16),
            pltpu.VMEM((NE * MAIN, WIDE), BF16),
            pltpu.VMEM((NE * 2 * REST, HALF), BF16),
            pltpu.VMEM((NE, 48, 128), BF16),
            pltpu.VMEM((ROWS, WIDE), BF16),
            pltpu.VMEM((NE * 2 * REST, HALF), BF16),
            pltpu.VMEM((ROWS, WIDE), BF16),
            pltpu.VMEM((NE * 2 * REST, HALF), BF16),
            pltpu.VMEM((NE, 48, 128), BF16),
            pltpu.VMEM((ROWS, FF), BF16),
            pltpu.VMEM((ROWS, FF), BF16),
            pltpu.VMEM((ROWS, FF), F32),
            pltpu.VMEM((ROWS, FF), F32),
            pltpu.VMEM((ROWS, FF), BF16),
            pltpu.VMEM((ROWS, FF), BF16),
            pltpu.VMEM((ROWS, 1), F32),
            pltpu.VMEM((ROWS, WIDE), BF16),
            pltpu.VMEM((NE * 2 * REST, HALF), BF16),
            pltpu.VMEM((NE, 48, 128), BF16),
            pltpu.VMEM((NE * MAIN, WIDE), BF16),
            pltpu.VMEM((NE * 2 * REST, HALF), BF16),
            pltpu.VMEM((NE, 48, 128), BF16),
            pltpu.VMEM((3, 2, NZ, 2, 64, FF), BF16),
            pltpu.VMEM((3, 2, NZ, 64, FF), BF16),
            pltpu.VMEM((3, 2, NZ, 64, FF), BF16),
            pltpu.VMEM((3, 64, FF), BF16),
            dma((9, NE)),
            dma((9, NE)),
            dma((3, 2, NZ)),
            dma((3, 2, NZ)),
            dma((3, 2, NZ - 1)),
            dma((3, 2, NZ - 1)),
            dma((3,)),
            dma((3,)),
        ],
        compiler_params=pltpu.CompilerParams(
            collective_id=0, has_side_effects=True, vmem_limit_bytes=56 * 2**20
        ),
        cost_estimate=pl.CostEstimate(
            flops=9 * 2 * ROWS * WIDE * FF, bytes_accessed=12 * 2**20, transcendentals=ROWS * FF
        ),
        name="moe_layer",
    )(slot_map, live, routes, probs, tokens, cotangent, wg, wu, wd)


def shards(tokens, cotangent, probs, routes, live, slot_map, w_gate, w_up, w_down):
    input_grad, prob_grad, down_share, gate_share, up_share = layer(
        slot_map,
        live,
        routes.T,
        probs.T.astype(F32),
        tokens,
        cotangent,
        w_gate[0],
        w_up[0],
        w_down[0],
    )
    return (
        input_grad,
        prob_grad.T.astype(BF16),
        gate_share[None],
        up_share[None],
        down_share.T[None],
    )


def solution(mesh):
    tok = P(("dp", "expert"), None)
    return jax.shard_map(
        shards,
        mesh=mesh,
        in_specs=(
            tok, tok, tok, tok,
            P(("dp", "expert")),
            P(),
            P("expert", None, None),
            P("expert", None, None),
            P("expert", None, None),
        ),
        out_specs=(
            tok,
            tok,
            P("expert", "dp", None),
            P("expert", "dp", None),
            P("expert", None, "dp"),
        ),
        check_vma=False,
    )
```

time: 492 us -> 120 us (0.24)
  waiting for transfers between devices: 366 us -> 0 us
  Pallas kernels: 0 us -> 110 us
  matrix products: 43.4 us -> 0 us
  starting transfers between devices: 23.7 us -> 0 us
  local copies, waits for them, and re-layouts: 27.8 us -> 6.73 us
  between operations: 13.9 us -> 0.64 us
  blocking collectives: 8.51 us -> 0 us
  other arithmetic: 7.59 us -> 2.4 us
    reduce_scatter x2 -> x0, waiting for transfers between devices: 248 us -> none  [the longest x1 124 us: shards(): lax.psum_scatter(grad_up[None].astype(jnp.bfloat16), 'dp', scatter_dimens...]
    pallas_call x0 -> x1, Pallas kernels: none -> 110 us  [layer(): pl.pallas_call(layer_kernel, out_shape=[jax.ShapeDtypeStruct((TOK, WIDE),...]
    unnamed x4 -> x0, waiting for transfers between devices: 80.1 us -> none
    dot_general x12 -> x0, matrix products: 43.4 us -> none  [the longest x4 17.5 us: contract_rows(): lax.dot_general(left, right, (((0,), (0,)), ((), ())), preferred_element_...]
    all_to_all x4 -> x0, waiting for transfers between devices: 38 us -> none  [the longest x1 13.2 us: shards(): lax.all_to_all(pair.reshape(groups, cap, width), 'expert', split_axis=0,...]
    all_to_all x4 -> x0, starting transfers between devices: 23.4 us -> none  [the longest x1 6.23 us: shards(): lax.all_to_all(pair.reshape(groups, cap, width), 'expert', split_axis=0,...]
    unnamed x20 -> x4, local copies, waits for them, and re-layouts: 25.2 us -> 6.73 us
    all_to_all x1 -> x0, blocking collectives: 8.51 us -> none  [shards(): lax.all_to_all(send_p, 'expert', split_axis=0, concat_axis=0, tiled=True)]
  transfers between devices with their start and end apart: 7 -> 0, of which waited for: 7 -> 0; matrix products, arithmetic and copies ran while one was open for 8% -> 0% of each run, Pallas kernels for 0% -> 0%
where the time goes in v2:
time: 120 us; the launch traced here: 119 us
  Pallas kernels  110 us (92%)
  local copies, waits for them, and re-layouts  6.73 us (6%)
  other arithmetic  2.4 us (2%)
    pallas_call x1, Pallas kernels, layer(): pl.pallas_call(layer_kernel, out_shape=[jax.ShapeDtypeStruct((TOK, WIDE),...  110 us
    unnamed x4, local copies, waits for them, and re-layouts  6.73 us

profile of v2, /device:TPU:24, one launch (start us, length us, event | category | flops | bytes accessed | tf_op | source)
XLA Modules:
  0.0 119.3 jit_solution(18267537278680484335)
XLA Ops:
  0.6 1.2 %convert_bitcast_fusion.probs_ref = f32[2,128]{1,0:T(2,128)} fusion(bf16[128,2]{0,1:T(2,128)(2,1)} %param.11), kind=kLoop, calls=%fused_computation | loop fusion | flops 256 | bytes 1536 | tf_op jit(solution)/shard_map/convert_element_type | solution.py:462
  1.9 109.5 %moe_layer.1 = (bf16[128,2048]{1,0:T(8,128)(2,1)}, f32[2,128]{1,0:T(2,128)}, f32[64,768]{1,0:T(8,128)}, f32[64,768]{1,0:T(8,128)}, f32[64,768]{1,0:T(8,128)}) custom-call(s32[8]{0:T(128)} %slot_ref.1, s32[2]{0:T(128)} %live_ref.1, s32[2,128]{1,0:T(2,128)} %bitcast.19, f32[2,128]{1,0:T(2,128)} %convert_bitcast_fusion.probs_ref, bf16[128,2048]{1,0:T(8,128)(2,1)} %tok_ref.1, ...), custom_call_target="tpu_custom_call" | custom-call | flops 9059696640 | bytes 12582912 | tf_op jit(solution)/shard_map/moe_layer/pallas_call | solution.py:393
  111.4 1.2 convert_bitcast_fusion.1
  112.6 1.9 %copy.18 = bf16[128,2048]{1,0:T(8,128)(2,1)} copy(bf16[128,2048]{1,0:T(8,128)(2,1)} %get-tuple-element.20) | data formatting | bytes 1048576
  114.4 1.6 %copy.19 = f32[1,64,768]{2,1,0:T(8,128)} copy(f32[1,64,768]{2,1,0:T(8,128)} %bitcast.15) | data formatting | bytes 393216
  116.1 1.6 %copy.20 = f32[1,64,768]{2,1,0:T(8,128)} copy(f32[1,64,768]{2,1,0:T(8,128)} %bitcast.14) | data formatting | bytes 393216
  117.7 1.6 %copy.21 = f32[1,768,64]{1,2,0:T(8,128)} copy(f32[1,768,64]{1,2,0:T(8,128)} %bitcast.13) | data formatting | bytes 393216

commit v3 on v2

--- a/solution.py
+++ b/solution.py
@@ -17,6 +17,8 @@
 REST = 8
 ROWS = NE * (MAIN + REST)
 LAST = NZ - 1
+GROUP = 2
+FIRST = NZ // GROUP
 
 
 def mm(a, b):
@@ -40,15 +42,15 @@
 
 
 def layer_kernel(
-    slot_ref, live_ref, routes_ref, probs_ref, tok_ref, cot_ref, wg_hbm, wu_hbm, wd_hbm,
+    slot_ref, live_ref, routes_ref, probs_ref, tok_hbm, cot_hbm, wg_hbm, wu_hbm, wd_hbm,
     in_ref, pg_ref, o_down, o_gate, o_up,
-    wg, wu, wd, w_sem,
+    tok_ref, cot_ref, wg, wu, wd, w_sem,
     pick, pick_a, pick_b, pick48,
-    sx, sxt, sdy, sdyt, sp, x, xt, dy, dyt, prob,
-    hid, phid, act1, act2, gg, ug, pp,
+    sx, sxt, sdy, sdyt, sp, x, xt, dy, dyt, prob, turned,
+    hid, phid, act1, act2, dyw, gg, ug,
     pair, pairt, sbp, back, backt, bp,
     grads, sib, ring, xbuf,
-    a2a_s, a2a_r, sib_s, sib_r, ring_s, ring_r, x_s, x_r,
+    a2a_s, a2a_r, dy_s, dy_r, sib_s, sib_r, ring_s, ring_r, x_s, x_r,
 ):
     dp = lax.axis_index("dp")
     me = lax.axis_index("expert")
@@ -58,20 +60,32 @@
     sibling = (xh * 16 + z * 2 + (1 - c), me)
     across = ((1 - xh) * 16 + z * 2 + c, me)
 
-    weights = [
+    loads = [
         pltpu.make_async_copy(src, dst, w_sem.at[i])
-        for i, (src, dst) in enumerate(((wg_hbm, wg), (wu_hbm, wu), (wd_hbm, wd)))
+        for i, (src, dst) in enumerate(
+            (
+                (tok_hbm, tok_ref),
+                (cot_hbm, cot_ref),
+                (wg_hbm, wg),
+                (wu_hbm, wu),
+                (wd_hbm, wd),
+            )
+        )
     ]
-    for w in weights:
-        w.start()
+    loads[0].start()
+
+    def partner(k):
+        return ((me // 4 + 1 - k // 4) % 2) * 4 + (me % 4 + k % 4 + k // 4) % 4
 
     barrier = pltpu.get_barrier_semaphore()
     for peer in (up, down, sibling, across):
         pl.semaphore_signal(barrier, inc=1, device_id=peer, device_id_type=MESH)
-    for k in range(1, NE):
+    for k in range(NE - 1):
         pl.semaphore_signal(
-            barrier, inc=1, device_id=(dp, (me + k) % NE), device_id_type=MESH
-        )
+            barrier, inc=1, device_id=(dp, partner(k)), device_id_type=MESH
+        )
+    for load in loads[1:]:
+        load.start()
 
     slot_iota = lax.broadcasted_iota(jnp.int32, (NE, TOK), 0)
     lane = lax.broadcasted_iota(jnp.int32, (1, TOK), 1)
@@ -103,19 +117,38 @@
         ((low == rests[0]) & (rests[0] >= 0)) | ((low == rests[1]) & (rests[1] >= 0))
     )
 
-    def dispatch(src, main, rest):
+    def dispatch():
         @pl.loop(0, 4)
         def _(n):
             cols = cols_at(n * 512, 512)
-            main[:, cols] = mm(pick[...], src[:, cols]).astype(BF16)
+            sx[:, cols] = mm(pick[...], tok_ref[:, cols]).astype(BF16)
 
         @pl.loop(0, 2)
         def _(n):
             cols = cols_at(n * 512, 512)
             more = cols_at(HALF + n * 512, 512)
-            rest[:, cols] = (
-                mm(pick_a[...], src[:, cols]) + mm(pick_b[...], src[:, more])
+            sxt[:, cols] = (
+                mm(pick_a[...], tok_ref[:, cols]) + mm(pick_b[...], tok_ref[:, more])
             ).astype(BF16)
+
+    def chunk(d, s):
+        return (z + 2 * NZ - 1 - s) % NZ if d == 0 else (z + 1 + s) % NZ
+
+    def step_cols(s):
+        return cols_at(chunk(0, s) * 128, 128), cols_at(HALF + chunk(1, s) * 128, 128)
+
+    def both(ref, s):
+        a, b = step_cols(s)
+        return jnp.concatenate([ref[:, a], ref[:, b]], 1)
+
+    def dispatch_cot():
+        @pl.loop(0, NZ)
+        def _(s):
+            a, b = step_cols(s)
+            sdy[s] = mm(pick[...], both(cot_ref, s)).astype(BF16)
+            sdyt[s] = (mm(pick_a[...], cot_ref[:, a]) + mm(pick_b[...], cot_ref[:, b])).astype(
+                BF16
+            )
 
     def piece(ref, kind, e):
         if kind % 3 == 0:
@@ -126,13 +159,13 @@
 
     exchanged = (
         (sx, x), (sxt, xt), (sp, prob),
-        (sdy, dy), (sdyt, dyt), None,
+        None, None, None,
         (pair, back), (pairt, backt), (sbp, bp),
     )
 
     def exchange(kind, k):
         src, dst = exchanged[kind]
-        to = (me + k) % NE
+        to = partner(k)
         return pltpu.make_async_remote_copy(
             src_ref=piece(src, kind, to),
             dst_ref=piece(dst, kind, me),
@@ -143,7 +176,7 @@
         )
 
     def start_all(kinds):
-        @pl.loop(1, NE)
+        @pl.loop(0, NE - 1)
         def _(k):
             for kind in kinds:
                 exchange(kind, k).start()
@@ -159,18 +192,32 @@
                 dst[rows, :] = src[rows, :]
 
     def wait_sent(kinds):
-        @pl.loop(1, NE)
+        @pl.loop(0, NE - 1)
         def _(k):
             for kind in kinds:
                 exchange(kind, k).wait_send()
 
     def wait_got(kinds):
-        @pl.loop(1, NE)
+        @pl.loop(0, NE - 1)
         def _(k):
             for kind in kinds:
                 exchange(kind, k).wait_recv()
 
-    dispatch(tok_ref, sx, sxt)
+    def dy_copy(kind, g, k):
+        to = partner(k)
+        steps = pl.ds(g * GROUP, GROUP)
+        src, dst, size = ((sdy, dy, MAIN), (sdyt, dyt, 2 * REST))[kind]
+        return pltpu.make_async_remote_copy(
+            src_ref=src.at[steps, pl.ds(pl.multiple_of(to * size, size), size)],
+            dst_ref=dst.at[steps, pl.ds(pl.multiple_of(me * size, size), size)],
+            send_sem=dy_s.at[kind, g, k],
+            recv_sem=dy_r.at[kind, g, k],
+            device_id=(dp, to),
+            device_id_type=MESH,
+        )
+
+    loads[0].wait()
+    dispatch()
     pl.semaphore_wait(barrier, 4 + NE - 1)
     start_all((0, 1))
     row = lax.broadcasted_iota(jnp.int32, (NE * 48, TOK), 0)
@@ -178,33 +225,40 @@
     for k in range(2):
         hit = jnp.where(row == alls[k], 1.0, 0.0)
         pick48[k] = hit
-        total += jnp.sum(hit * probs_ref[k : k + 1, :], 1, keepdims=True)
+        total += jnp.sum(hit * probs_ref[k : k + 1, :].astype(F32), 1, keepdims=True)
     sp[...] = jnp.broadcast_to(total, (NE * 48, 128)).astype(BF16).reshape(NE, 48, 128)
     keep_own((0, 1, 2))
-    dispatch(cot_ref, sdy, sdyt)
-    keep_own((3, 4))
-    wait_sent((0, 1))
-    start_all((3, 4, 2))
+    loads[1].wait()
+    dispatch_cot()
+    for size, src, dst in ((MAIN, sdy, dy), (2 * REST, sdyt, dyt)):
+        rows = pl.ds(pl.multiple_of(me * size, size), size)
+        dst[:, rows, :] = src[:, rows, :]
+    start_all((2,))
+
+    @pl.loop(0, NZ // GROUP)
+    def _(g):
+        @pl.loop(0, NE - 1)
+        def _(k):
+            for kind in range(2):
+                dy_copy(kind, g, k).start()
 
     part = lax.broadcasted_iota(jnp.int32, (NE * REST, NE * 2 * REST), 0)
     from_row = lax.broadcasted_iota(jnp.int32, (NE * REST, NE * 2 * REST), 1)
     first = (part // REST) * 2 * REST + part % REST
     take_a, take_b = one_hot(from_row == first), one_hot(from_row == first + REST)
 
-    def join(main, rest):
-        rows = pl.ds(NE * MAIN, NE * REST)
-
-        @pl.loop(0, 2)
-        def _(n):
-            cols = cols_at(n * 512, 512)
-            half = rest[:, cols]
-            main[rows, cols] = mm(take_a, half).astype(BF16)
-            main[rows, cols_at(HALF + n * 512, 512)] = mm(take_b, half).astype(BF16)
-
+    rest_rows = pl.ds(NE * MAIN, NE * REST)
     wait_got((0, 1))
-    join(x, xt)
-    weights[0].wait()
-    weights[1].wait()
+
+    @pl.loop(0, 2)
+    def _(n):
+        cols = cols_at(n * 512, 512)
+        half = xt[:, cols]
+        x[rest_rows, cols] = mm(take_a, half).astype(BF16)
+        x[rest_rows, cols_at(HALF + n * 512, 512)] = mm(take_b, half).astype(BF16)
+
+    loads[2].wait()
+    loads[3].wait()
 
     @pl.loop(0, FF // 256)
     def _(n):
@@ -217,7 +271,7 @@
         act1[:, cols] = u * sig * (1.0 + gate * (1.0 - sig))
         act2[:, cols] = gs
 
-    weights[2].wait()
+    loads[4].wait()
     wait_got((2,))
     p_all = prob[...].astype(F32)
     weight = jnp.concatenate(
@@ -228,11 +282,6 @@
         0,
     )[:, :1]
     phid[...] = (weight * hid[...].astype(F32)).astype(BF16)
-    wait_got((3, 4))
-    join(dy, dyt)
-
-    def chunk(d, s):
-        return (z + 2 * NZ - 1 - s) % NZ if d == 0 else (z + 1 + s) % NZ
 
     def sib_copy(m, d, s):
         at = chunk(d, s)
@@ -268,21 +317,10 @@
     def own(m, d, at):
         return grads[m, d, at, c].astype(F32) + sib[m, d, at].astype(F32)
 
-    def make_grads(left, rights):
-        @pl.loop(0, NZ)
-        def _(s):
-            lhs = jnp.concatenate(
-                [
-                    left[:, cols_at(chunk(0, s) * 128, 128)],
-                    left[:, cols_at(HALF + chunk(1, s) * 128, 128)],
-                ],
-                1,
-            )
-            for m, right in rights:
-                out = mm_tn(lhs, right[...]).astype(BF16)
-                for d in range(2):
-                    grads[m, d, chunk(d, s)] = out[d * 128 : d * 128 + 128].reshape(2, 64, FF)
-                    sib_copy(m, d, s).start()
+    def put_grads(m, s, out):
+        for d in range(2):
+            grads[m, d, chunk(d, s)] = out[d * 128 : d * 128 + 128].reshape(2, 64, FF)
+            sib_copy(m, d, s).start()
 
     def ring_start(m):
         for d in range(2):
@@ -306,42 +344,74 @@
         ).astype(BF16)
         x_copy(m).start()
 
-    make_grads(dy, ((0, phid),))
-    ring_start(0)
-
-    pp[...] = jnp.zeros_like(pp)
-
-    @pl.loop(0, FF // 256)
-    def _(n):
-        cols = cols_at(n * 256, 256)
-        dyw = mm_nt(dy[...], wd[cols, :])
-        pp[...] += jnp.sum(hid[:, cols].astype(F32) * dyw, 1, keepdims=True)
-        hg = dyw * weight
+    dyw[...] = jnp.zeros_like(dyw)
+    for g in range(NZ // GROUP):
+
+        @pl.loop(0, NE - 1)
+        def _(k):
+            for kind in range(2):
+                dy_copy(kind, g, k).wait_recv()
+
+        @pl.loop(g * GROUP, g * GROUP + GROUP)
+        def _(s):
+            half = dyt[s]
+            dy[s, rest_rows, :128] = mm(take_a, half).astype(BF16)
+            dy[s, rest_rows, 128:] = mm(take_b, half).astype(BF16)
+            put_grads(0, s, mm_tn(dy[s], phid[...]).astype(BF16))
+
+        @pl.loop(g * GROUP, g * GROUP + GROUP)
+        def _(s):
+            dyw[...] += mm_nt(dy[s], both(wd, s))
+            turned[s] = both(x, s).T
+
+        if g == 0:
+            ring_start(0)
+        elif g < FIRST - 1:
+            ring_step(0, g)
+
+    total = jnp.zeros((ROWS, 1), F32)
+    for n in range(FF // 256):
+        cols = pl.ds(n * 256, 256)
+        part = dyw[:, cols]
+        total += jnp.sum(hid[:, cols].astype(F32) * part, 1, keepdims=True)
+        hg = part * weight
         gg[:, cols] = (hg * act1[:, cols]).astype(BF16)
         ug[:, cols] = (hg * act2[:, cols]).astype(BF16)
 
-    ring_step(0, 1)
-    make_grads(x, ((1, gg), (2, ug)))
-    ring_start(1)
-    ring_start(2)
-    ring_step(0, 2)
-
-    @pl.loop(0, WIDE // 256)
-    def _(n):
+    for m, right in ((1, gg), (2, ug)):
+
+        @pl.loop(0, NZ)
+        def _(s):
+            put_grads(m, s, mm(turned[s], right[...]).astype(BF16))
+
+        ring_start(m)
+
+    def pair_cols(n):
         cols = cols_at(n * 256, 256)
         pair[:, cols] = (mm_nt(gg[...], wg[cols, :]) + mm_nt(ug[...], wu[cols, :])).astype(BF16)
 
-    rows = pl.ds(NE * MAIN, NE * REST)
+    pair_cols(0)
+    ring_step(0, FIRST - 1)
+    pair_cols(1)
+
+    @pl.loop(1, 3)
+    def _(s):
+        ring_step(1, s)
+        pair_cols(3 * s - 1)
+        ring_step(2, s)
+        pair_cols(3 * s)
+        ring_step(0, s + FIRST - 1)
+        pair_cols(3 * s + 1)
 
     @pl.loop(0, 2)
     def _(n):
         cols = cols_at(n * 512, 512)
         pairt[:, cols] = (
-            mm_tn(take_a, pair[rows, cols])
-            + mm_tn(take_b, pair[rows, cols_at(HALF + n * 512, 512)])
+            mm_tn(take_a, pair[rest_rows, cols])
+            + mm_tn(take_b, pair[rest_rows, cols_at(HALF + n * 512, 512)])
         ).astype(BF16)
 
-    part = jnp.broadcast_to(pp[...], (ROWS, 128))
+    part = jnp.broadcast_to(total, (ROWS, 128))
     sbp[:, :MAIN] = part[: NE * MAIN].reshape(NE, MAIN, 128).astype(BF16)
     sbp[:, MAIN:] = jnp.concatenate(
         [part[NE * MAIN :].reshape(NE, REST, 128), jnp.zeros((NE, REST, 128), F32)], 1
@@ -349,17 +419,15 @@
     start_all((6, 7, 8))
     keep_own((6, 7, 8))
 
-    @pl.loop(1, 5)
-    def _(s):
+    ring_step(1, 3)
+    ring_step(2, 3)
+    ring_step(0, LAST - 1)
+
+    for s in range(LAST - FIRST + 1, LAST):
         ring_step(1, s)
         ring_step(2, s)
-        ring_step(0, s + 2)
-
-    ring_step(1, 5)
-    ring_step(2, 5)
-    ring_end(0)
-    ring_step(1, 6)
-    ring_step(2, 6)
+        if s == LAST - FIRST + 1:
+            ring_end(0)
 
     wait_got((6, 7, 8))
 
@@ -376,55 +444,71 @@
 
     parts = bp[...].astype(F32).reshape(NE * 48, 128)
     for k in range(2):
-        pg_ref[k : k + 1, :] = jnp.sum(pick48[k] * parts, 0, keepdims=True)
+        pg_ref[k : k + 1, :] = jnp.sum(pick48[k] * parts, 0, keepdims=True).astype(BF16)
 
     ring_end(1)
     ring_end(2)
     for m, out in enumerate((o_down, o_gate, o_up)):
         x_copy(m).wait()
         out[...] = ring[m, xh, LAST].astype(F32) + own(m, xh, z) + xbuf[m].astype(F32)
-    wait_sent((2, 3, 4, 6, 7, 8))
+    wait_sent((0, 1, 2, 6, 7, 8))
+
+    @pl.loop(0, NZ // GROUP)
+    def _(g):
+        @pl.loop(0, NE - 1)
+        def _(k):
+            for kind in range(2):
+                dy_copy(kind, g, k).wait_send()
+
+
+def hand_over(*refs):
+    half = len(refs) // 2
+    for src, dst in zip(refs[:half], refs[half:]):
+        dst[...] = src[...]
 
 
 def layer(slot_map, live, routes, probs, tokens, cotangent, wg, wu, wd):
     vmem, smem = pl.BlockSpec(memory_space=pltpu.VMEM), pl.BlockSpec(memory_space=pltpu.SMEM)
     anywhere = pl.BlockSpec(memory_space=pl.ANY)
     dma = pltpu.SemaphoreType.DMA
-    return pl.pallas_call(
+    shapes = [
+        jax.ShapeDtypeStruct((TOK, WIDE), BF16),
+        jax.ShapeDtypeStruct((2, TOK), BF16),
+    ] + [jax.ShapeDtypeStruct((64, FF), F32)] * 3
+    results = pl.pallas_call(
         layer_kernel,
-        out_shape=[
-            jax.ShapeDtypeStruct((TOK, WIDE), BF16),
-            jax.ShapeDtypeStruct((2, TOK), F32),
-        ]
-        + [jax.ShapeDtypeStruct((64, FF), F32)] * 3,
-        in_specs=[smem, smem, vmem, vmem, vmem, vmem, anywhere, anywhere, anywhere],
+        out_shape=shapes,
+        in_specs=[smem, smem, vmem, vmem] + [anywhere] * 5,
         out_specs=[vmem] * 5,
         scratch_shapes=[
+            pltpu.VMEM((TOK, WIDE), BF16),
+            pltpu.VMEM((TOK, WIDE), BF16),
             pltpu.VMEM((WIDE, FF), BF16),
             pltpu.VMEM((WIDE, FF), BF16),
             pltpu.VMEM((FF, WIDE), BF16),
-            dma((3,)),
+            dma((5,)),
             pltpu.VMEM((NE * MAIN, TOK), BF16),
             pltpu.VMEM((NE * 2 * REST, TOK), BF16),
             pltpu.VMEM((NE * 2 * REST, TOK), BF16),
             pltpu.VMEM((2, NE * 48, TOK), F32),
             pltpu.VMEM((NE * MAIN, WIDE), BF16),
             pltpu.VMEM((NE * 2 * REST, HALF), BF16),
-            pltpu.VMEM((NE * MAIN, WIDE), BF16),
-            pltpu.VMEM((NE * 2 * REST, HALF), BF16),
+            pltpu.VMEM((NZ, NE * MAIN, 256), BF16),
+            pltpu.VMEM((NZ, NE * 2 * REST, 128), BF16),
             pltpu.VMEM((NE, 48, 128), BF16),
             pltpu.VMEM((ROWS, WIDE), BF16),
             pltpu.VMEM((NE * 2 * REST, HALF), BF16),
-            pltpu.VMEM((ROWS, WIDE), BF16),
-            pltpu.VMEM((NE * 2 * REST, HALF), BF16),
+            pltpu.VMEM((NZ, ROWS, 256), BF16),
+            pltpu.VMEM((NZ, NE * 2 * REST, 128), BF16),
             pltpu.VMEM((NE, 48, 128), BF16),
+            pltpu.VMEM((NZ, 256, ROWS), BF16),
             pltpu.VMEM((ROWS, FF), BF16),
             pltpu.VMEM((ROWS, FF), BF16),
             pltpu.VMEM((ROWS, FF), F32),
             pltpu.VMEM((ROWS, FF), F32),
+            pltpu.VMEM((ROWS, FF), F32),
             pltpu.VMEM((ROWS, FF), BF16),
             pltpu.VMEM((ROWS, FF), BF16),
-            pltpu.VMEM((ROWS, 1), F32),
             pltpu.VMEM((ROWS, WIDE), BF16),
             pltpu.VMEM((NE * 2 * REST, HALF), BF16),
             pltpu.VMEM((NE, 48, 128), BF16),
@@ -437,6 +521,8 @@
             pltpu.VMEM((3, 64, FF), BF16),
             dma((9, NE)),
             dma((9, NE)),
+            dma((2, NZ // GROUP, NE)),
+            dma((2, NZ // GROUP, NE)),
             dma((3, 2, NZ)),
             dma((3, 2, NZ)),
             dma((3, 2, NZ - 1)),
@@ -452,6 +538,13 @@
         ),
         name="moe_layer",
     )(slot_map, live, routes, probs, tokens, cotangent, wg, wu, wd)
+    return pl.pallas_call(
+        hand_over,
+        out_shape=shapes,
+        in_specs=[vmem] * 5,
+        out_specs=[vmem] * 5,
+        name="hand_over",
+    )(*results)
 
 
 def shards(tokens, cotangent, probs, routes, live, slot_map, w_gate, w_up, w_down):
@@ -459,7 +552,7 @@
         slot_map,
         live,
         routes.T,
-        probs.T.astype(F32),
+        probs.T,
         tokens,
         cotangent,
         w_gate[0],
@@ -468,7 +561,7 @@
     )
     return (
         input_grad,
-        prob_grad.T.astype(BF16),
+        prob_grad.T,
         gate_share[None],
         up_share[None],
         down_share.T[None],

time: 120 us -> 103 us (0.86)
  Pallas kernels: 110 us -> 101 us
  local copies, waits for them, and re-layouts: 6.73 us -> 0 us
  other arithmetic: 2.4 us -> 0 us
    pallas_call x1 -> x2, Pallas kernels: 110 us -> 101 us  [the longest x1 98.7 us: layer(): pl.pallas_call(layer_kernel, out_shape=shapes, in_specs=[smem, smem, vmem...]
    unnamed x4 -> x0, local copies, waits for them, and re-layouts: 6.73 us -> none
    convert_element_type x2 -> x0, other arithmetic: 2.4 us -> none  [the longest x1 1.22 us: shards(): probs.T.astype(F32)]
where the time goes in v3:
time: 103 us; the launch traced here: 102 us
  Pallas kernels  101 us (98%)
    pallas_call x1, Pallas kernels, layer(): pl.pallas_call(layer_kernel, out_shape=shapes, in_specs=[smem, smem, vmem...  98.7 us
    pallas_call x1, Pallas kernels, layer(): pl.pallas_call(hand_over, out_shape=shapes, in_specs=[vmem] * 5, out_spec...  2.25 us

profile of v3, /device:TPU:24, one launch (start us, length us, event | category | flops | bytes accessed | tf_op | source)
XLA Modules:
  0.0 101.6 jit_solution(16724237380394112874)
XLA Ops:
  0.6 98.7 %moe_layer.1 = (bf16[128,2048]{1,0:T(8,128)(2,1)}, bf16[2,128]{1,0:T(2,128)(2,1)}, f32[64,768]{1,0:T(8,128)}, f32[64,768]{1,0:T(8,128)}, f32[64,768]{1,0:T(8,128)}) custom-call(s32[8]{0:T(128)} %slot_ref.1, s32[2]{0:T(128)} %live_ref.1, s32[2,128]{1,0:T(2,128)} %bitcast.17, bf16[2,128]{1,0:T(2,128)(2,1)} %bitcast.18, bf16[128,2048]{1,0:T(8,128)(2,1)} %tok_hbm.1, ...), custom_call_target="tpu_custom_call" | custom-call | flops 9059696640 | bytes 12582912 | tf_op jit(solution)/shard_map/moe_layer/pallas_call | solution.py:478
  99.3 2.2 %hand_over.1 = (bf16[128,2048]{1,0:T(8,128)(2,1)}, bf16[2,128]{1,0:T(2,128)(2,1)}, f32[64,768]{1,0:T(8,128)}, f32[64,768]{1,0:T(8,128)}, f32[64,768]{1,0:T(8,128)}) custom-call(bf16[128,2048]{1,0:T(8,128)(2,1)} %get-tuple-element.15.refs_0_, bf16[2,128]{1,0:T(2,128)(2,1)} %get-tuple-element.16.refs_1_, f32[64,768]{1,0:T(8,128)} %get-tuple-element.17.refs_2_, ...), custom_call_target="tpu_custom_call" | custom-call | tf_op jit(solution)/shard_map/hand_over/pallas_call | solution.py:541

commit v4 on v3

--- a/solution.py
+++ b/solution.py
@@ -18,7 +18,7 @@
 ROWS = NE * (MAIN + REST)
 LAST = NZ - 1
 GROUP = 2
-FIRST = NZ // GROUP
+ROUNDS = NZ // GROUP
 
 
 def mm(a, b):
@@ -132,7 +132,9 @@
             ).astype(BF16)
 
     def chunk(d, s):
-        return (z + 2 * NZ - 1 - s) % NZ if d == 0 else (z + 1 + s) % NZ
+        r, short = s // 2, s % 2
+        ahead = (4 - r) * (1 - short) + (5 + r) * short
+        return (z + ahead) % NZ if d == 0 else (z + 2 * NZ - ahead) % NZ
 
     def step_cols(s):
         return cols_at(chunk(0, s) * 128, 128), cols_at(HALF + chunk(1, s) * 128, 128)
@@ -235,7 +237,7 @@
         dst[:, rows, :] = src[:, rows, :]
     start_all((2,))
 
-    @pl.loop(0, NZ // GROUP)
+    @pl.loop(0, ROUNDS)
     def _(g):
         @pl.loop(0, NE - 1)
         def _(k):
@@ -294,19 +296,22 @@
             device_id_type=MESH,
         )
 
-    def ring_copy(m, d, s):
+    def toward(d, short):
+        return up if d == short else down
+
+    def ring_copy(m, d, short, r):
         return pltpu.make_async_remote_copy(
-            src_ref=ring.at[m, d, s],
-            dst_ref=ring.at[m, d, s + 1],
-            send_sem=ring_s.at[m, d, s],
-            recv_sem=ring_r.at[m, d, s],
-            device_id=up if d == 0 else down,
+            src_ref=ring.at[m, d, short, r],
+            dst_ref=ring.at[m, d, short, r + 1],
+            send_sem=ring_s.at[m, d, short, r],
+            recv_sem=ring_r.at[m, d, short, r],
+            device_id=toward(d, short),
             device_id_type=MESH,
         )
 
     def x_copy(m):
         return pltpu.make_async_remote_copy(
-            src_ref=ring.at[m, 1 - xh, LAST],
+            src_ref=ring.at[m, 1 - xh, 0, ROUNDS],
             dst_ref=xbuf.at[m],
             send_sem=x_s.at[m],
             recv_sem=x_r.at[m],
@@ -314,6 +319,9 @@
             device_id_type=MESH,
         )
 
+    def flows(r):
+        return [(d, short) for short in range(2 if r < ROUNDS - 1 else 1) for d in range(2)]
+
     def own(m, d, at):
         return grads[m, d, at, c].astype(F32) + sib[m, d, at].astype(F32)
 
@@ -322,30 +330,32 @@
             grads[m, d, chunk(d, s)] = out[d * 128 : d * 128 + 128].reshape(2, 64, FF)
             sib_copy(m, d, s).start()
 
-    def ring_start(m):
-        for d in range(2):
-            sib_copy(m, d, 0).wait()
-            ring[m, d, 0] = own(m, d, chunk(d, 0)).astype(BF16)
-            ring_copy(m, d, 0).start()
-
-    def ring_step(m, s):
-        for d in range(2):
+    def ring_step(m, r):
+        for d, short in flows(r):
+            s = 2 * r + short
             sib_copy(m, d, s).wait()
-            ring_copy(m, d, s - 1).wait()
-            ring[m, d, s] = (ring[m, d, s].astype(F32) + own(m, d, chunk(d, s))).astype(BF16)
-            ring_copy(m, d, s).start()
+            term = own(m, d, chunk(d, s))
+            if r > 0:
+                ring_copy(m, d, short, r - 1).wait()
+                term += ring[m, d, short, r].astype(F32)
+            ring[m, d, short, r] = term.astype(BF16)
+            ring_copy(m, d, short, r).start()
+
+    def ring_total(m, d):
+        return (
+            ring[m, d, 0, ROUNDS].astype(F32) + ring[m, d, 1, ROUNDS - 1].astype(F32) + own(m, d, z)
+        )
 
     def ring_end(m):
         for d in range(2):
             sib_copy(m, d, LAST).wait()
-            ring_copy(m, d, LAST - 1).wait()
-        ring[m, 1 - xh, LAST] = (
-            ring[m, 1 - xh, LAST].astype(F32) + own(m, 1 - xh, z)
-        ).astype(BF16)
+            ring_copy(m, d, 0, ROUNDS - 1).wait()
+            ring_copy(m, d, 1, ROUNDS - 2).wait()
+        ring[m, 1 - xh, 0, ROUNDS] = ring_total(m, 1 - xh).astype(BF16)
         x_copy(m).start()
 
     dyw[...] = jnp.zeros_like(dyw)
-    for g in range(NZ // GROUP):
+    for g in range(ROUNDS):
 
         @pl.loop(0, NE - 1)
         def _(k):
@@ -364,9 +374,7 @@
             dyw[...] += mm_nt(dy[s], both(wd, s))
             turned[s] = both(x, s).T
 
-        if g == 0:
-            ring_start(0)
-        elif g < FIRST - 1:
+        if g < ROUNDS - 1:
             ring_step(0, g)
 
     total = jnp.zeros((ROWS, 1), F32)
@@ -384,24 +392,15 @@
         def _(s):
             put_grads(m, s, mm(turned[s], right[...]).astype(BF16))
 
-        ring_start(m)
+        ring_step(m, 0)
+        if m == 1:
+            ring_step(0, ROUNDS - 1)
 
     def pair_cols(n):
         cols = cols_at(n * 256, 256)
         pair[:, cols] = (mm_nt(gg[...], wg[cols, :]) + mm_nt(ug[...], wu[cols, :])).astype(BF16)
 
-    pair_cols(0)
-    ring_step(0, FIRST - 1)
-    pair_cols(1)
-
-    @pl.loop(1, 3)
-    def _(s):
-        ring_step(1, s)
-        pair_cols(3 * s - 1)
-        ring_step(2, s)
-        pair_cols(3 * s)
-        ring_step(0, s + FIRST - 1)
-        pair_cols(3 * s + 1)
+    pl.loop(0, 8)(pair_cols)
 
     @pl.loop(0, 2)
     def _(n):
@@ -419,16 +418,14 @@
     start_all((6, 7, 8))
     keep_own((6, 7, 8))
 
-    ring_step(1, 3)
-    ring_step(2, 3)
-    ring_step(0, LAST - 1)
-
-    for s in range(LAST - FIRST + 1, LAST):
-        ring_step(1, s)
-        ring_step(2, s)
-        if s == LAST - FIRST + 1:
+    for r in range(1, ROUNDS):
+        ring_step(1, r)
+        ring_step(2, r)
+        if r == 1:
             ring_end(0)
 
+    ring_end(1)
+    ring_end(2)
     wait_got((6, 7, 8))
 
     @pl.loop(0, 2)
@@ -446,14 +443,12 @@
     for k in range(2):
         pg_ref[k : k + 1, :] = jnp.sum(pick48[k] * parts, 0, keepdims=True).astype(BF16)
 
-    ring_end(1)
-    ring_end(2)
     for m, out in enumerate((o_down, o_gate, o_up)):
         x_copy(m).wait()
-        out[...] = ring[m, xh, LAST].astype(F32) + own(m, xh, z) + xbuf[m].astype(F32)
+        out[...] = ring_total(m, xh) + xbuf[m].astype(F32)
     wait_sent((0, 1, 2, 6, 7, 8))
 
-    @pl.loop(0, NZ // GROUP)
+    @pl.loop(0, ROUNDS)
     def _(g):
         @pl.loop(0, NE - 1)
         def _(k):
@@ -517,16 +512,16 @@
             pltpu.VMEM((NE, 48, 128), BF16),
             pltpu.VMEM((3, 2, NZ, 2, 64, FF), BF16),
             pltpu.VMEM((3, 2, NZ, 64, FF), BF16),
-            pltpu.VMEM((3, 2, NZ, 64, FF), BF16),
+            pltpu.VMEM((3, 2, 2, ROUNDS + 1, 64, FF), BF16),
             pltpu.VMEM((3, 64, FF), BF16),
             dma((9, NE)),
             dma((9, NE)),
-            dma((2, NZ // GROUP, NE)),
-            dma((2, NZ // GROUP, NE)),
+            dma((2, ROUNDS, NE)),
+            dma((2, ROUNDS, NE)),
             dma((3, 2, NZ)),
             dma((3, 2, NZ)),
-            dma((3, 2, NZ - 1)),
-            dma((3, 2, NZ - 1)),
+            dma((3, 2, 2, ROUNDS)),
+            dma((3, 2, 2, ROUNDS)),
             dma((3,)),
             dma((3,)),
         ],

time: 103 us -> 95.6 us (0.928)
  Pallas kernels: 101 us -> 94.1 us
    pallas_call x1, Pallas kernels: 98.7 us -> 91.8 us  [layer(): pl.pallas_call(layer_kernel, out_shape=shapes, in_specs=[smem, smem, vmem...]
where the time goes in v4:
time: 95.6 us; the launch traced here: 94.7 us
  Pallas kernels  94.1 us (98%)
    pallas_call x1, Pallas kernels, layer(): pl.pallas_call(layer_kernel, out_shape=shapes, in_specs=[smem, smem, vmem...  91.8 us
    pallas_call x1, Pallas kernels, layer(): pl.pallas_call(hand_over, out_shape=shapes, in_specs=[vmem] * 5, out_spec...  2.25 us

profile of v4, /device:TPU:24, one launch (start us, length us, event | category | flops | bytes accessed | tf_op | source)
XLA Modules:
  0.0 94.7 jit_solution(17067276857043481187)
XLA Ops:
  0.6 91.8 %moe_layer.1 = (bf16[128,2048]{1,0:T(8,128)(2,1)}, bf16[2,128]{1,0:T(2,128)(2,1)}, f32[64,768]{1,0:T(8,128)}, f32[64,768]{1,0:T(8,128)}, f32[64,768]{1,0:T(8,128)}) custom-call(s32[8]{0:T(128)} %slot_ref.1, s32[2]{0:T(128)} %live_ref.1, s32[2,128]{1,0:T(2,128)} %bitcast.17, bf16[2,128]{1,0:T(2,128)(2,1)} %bitcast.18, bf16[128,2048]{1,0:T(8,128)(2,1)} %tok_hbm.1, ...), custom_call_target="tpu_custom_call" | custom-call | flops 9059696640 | bytes 12582912 | tf_op jit(solution)/shard_map/moe_layer/pallas_call | solution.py:473
  92.5 2.2 %hand_over.1 = (bf16[128,2048]{1,0:T(8,128)(2,1)}, bf16[2,128]{1,0:T(2,128)(2,1)}, f32[64,768]{1,0:T(8,128)}, f32[64,768]{1,0:T(8,128)}, f32[64,768]{1,0:T(8,128)}) custom-call(bf16[128,2048]{1,0:T(8,128)(2,1)} %get-tuple-element.15.refs_0_, bf16[2,128]{1,0:T(2,128)(2,1)} %get-tuple-element.16.refs_1_, f32[64,768]{1,0:T(8,128)} %get-tuple-element.17.refs_2_, ...), custom_call_target="tpu_custom_call" | custom-call | tf_op jit(solution)/shard_map/hand_over/pallas_call | solution.py:536

commit v5 on v4

--- a/solution.py
+++ b/solution.py
@@ -42,8 +42,10 @@
 
 
 def layer_kernel(
-    slot_ref, live_ref, routes_ref, probs_ref, tok_hbm, cot_hbm, wg_hbm, wu_hbm, wd_hbm,
-    in_ref, pg_ref, o_down, o_gate, o_up,
+    slot_hbm, live_hbm, routes_hbm, probs_hbm, tok_hbm, cot_hbm, wg_hbm, wu_hbm, wd_hbm,
+    in_out, pg_out, down_out, gate_out, up_out,
+    in_ref, pg_ref, o_down, o_gate, o_up, out_sem,
+    slot_ref, live_ref, routes_ref, probs_ref, small_sem,
     tok_ref, cot_ref, wg, wu, wd, w_sem,
     pick, pick_a, pick_b, pick48,
     sx, sxt, sdy, sdyt, sp, x, xt, dy, dyt, prob, turned,
@@ -72,7 +74,21 @@
             )
         )
     ]
+    small = [
+        pltpu.make_async_copy(src, dst, small_sem.at[i])
+        for i, (src, dst) in enumerate(
+            (
+                (slot_hbm, slot_ref),
+                (live_hbm, live_ref),
+                (routes_hbm, routes_ref),
+                (probs_hbm, probs_ref),
+            )
+        )
+    ]
+    for load in small:
+        load.start()
     loads[0].start()
+
 
     def partner(k):
         return ((me // 4 + 1 - k // 4) % 2) * 4 + (me % 4 + k % 4 + k // 4) % 4
@@ -86,6 +102,8 @@
         )
     for load in loads[1:]:
         load.start()
+    for load in small:
+        load.wait()
 
     slot_iota = lax.broadcasted_iota(jnp.int32, (NE, TOK), 0)
     lane = lax.broadcasted_iota(jnp.int32, (1, TOK), 1)
@@ -424,6 +442,18 @@
         if r == 1:
             ring_end(0)
 
+    results = [
+        pltpu.make_async_copy(src, dst, out_sem.at[i])
+        for i, (src, dst) in enumerate(
+            (
+                (o_down, down_out),
+                (o_gate, gate_out),
+                (o_up, up_out),
+                (in_ref, in_out),
+                (pg_ref, pg_out),
+            )
+        )
+    ]
     ring_end(1)
     ring_end(2)
     wait_got((6, 7, 8))
@@ -443,9 +473,14 @@
     for k in range(2):
         pg_ref[k : k + 1, :] = jnp.sum(pick48[k] * parts, 0, keepdims=True).astype(BF16)
 
+    results[3].start()
+    results[4].start()
     for m, out in enumerate((o_down, o_gate, o_up)):
         x_copy(m).wait()
         out[...] = ring_total(m, xh) + xbuf[m].astype(F32)
+        results[m].start()
+    for result in results:
+        result.wait()
     wait_sent((0, 1, 2, 6, 7, 8))
 
     @pl.loop(0, ROUNDS)
@@ -457,13 +492,19 @@
 
 
 def hand_over(*refs):
-    half = len(refs) // 2
-    for src, dst in zip(refs[:half], refs[half:]):
-        dst[...] = src[...]
+    srcs, dsts, held, sems = refs[:5], refs[5:10], refs[10:15], refs[15]
+    loads = [pltpu.make_async_copy(a, b, sems.at[0, i]) for i, (a, b) in enumerate(zip(srcs, held))]
+    stores = [pltpu.make_async_copy(a, b, sems.at[1, i]) for i, (a, b) in enumerate(zip(held, dsts))]
+    for load in loads:
+        load.start()
+    for load, store in zip(loads, stores):
+        load.wait()
+        store.start()
+    for store in stores:
+        store.wait()
 
 
 def layer(slot_map, live, routes, probs, tokens, cotangent, wg, wu, wd):
-    vmem, smem = pl.BlockSpec(memory_space=pltpu.VMEM), pl.BlockSpec(memory_space=pltpu.SMEM)
     anywhere = pl.BlockSpec(memory_space=pl.ANY)
     dma = pltpu.SemaphoreType.DMA
     shapes = [
@@ -473,9 +514,16 @@
     results = pl.pallas_call(
         layer_kernel,
         out_shape=shapes,
-        in_specs=[smem, smem, vmem, vmem] + [anywhere] * 5,
-        out_specs=[vmem] * 5,
-        scratch_shapes=[
+        in_specs=[anywhere] * 9,
+        out_specs=[anywhere] * 5,
+        scratch_shapes=[pltpu.VMEM(shape.shape, shape.dtype) for shape in shapes]
+        + [
+            dma((5,)),
+            pltpu.SMEM((NE,), jnp.int32),
+            pltpu.SMEM((2,), jnp.int32),
+            pltpu.VMEM((2, TOK), jnp.int32),
+            pltpu.VMEM((2, TOK), BF16),
+            dma((4,)),
             pltpu.VMEM((TOK, WIDE), BF16),
             pltpu.VMEM((TOK, WIDE), BF16),
             pltpu.VMEM((WIDE, FF), BF16),
@@ -536,8 +584,9 @@
     return pl.pallas_call(
         hand_over,
         out_shape=shapes,
-        in_specs=[vmem] * 5,
-        out_specs=[vmem] * 5,
+        in_specs=[anywhere] * 5,
+        out_specs=[anywhere] * 5,
+        scratch_shapes=[pltpu.VMEM(shape.shape, shape.dtype) for shape in shapes] + [dma((2, 5))],
         name="hand_over",
     )(*results)
 

time: 95.6 us -> 94.5 us (0.988)
  Pallas kernels: 94.1 us -> 93 us
    pallas_call x2, Pallas kernels: 94.1 us -> 93 us  [the longest x1 90.9 us: layer(): pl.pallas_call(layer_kernel, out_shape=shapes, in_specs=[anywhere] * 9, o...]
where the time goes in v5:
time: 94.5 us; the launch traced here: 93.7 us
  Pallas kernels  93 us (98%)
    pallas_call x1, Pallas kernels, layer(): pl.pallas_call(layer_kernel, out_shape=shapes, in_specs=[anywhere] * 9, o...  90.9 us
    pallas_call x1, Pallas kernels, layer(): pl.pallas_call(hand_over, out_shape=shapes, in_specs=[anywhere] * 5, out_...  2.11 us

profile of v5, /device:TPU:24, one launch (start us, length us, event | category | flops | bytes accessed | tf_op | source)
XLA Modules:
  0.0 93.7 jit_solution(2486687691232464321)
XLA Ops:
  0.6 90.9 %moe_layer.1 = (bf16[128,2048]{1,0:T(8,128)(2,1)}, bf16[2,128]{1,0:T(2,128)(2,1)}, f32[64,768]{1,0:T(8,128)}, f32[64,768]{1,0:T(8,128)}, f32[64,768]{1,0:T(8,128)}) custom-call(s32[8]{0:T(128)} %slot_hbm.1, s32[2]{0:T(128)} %live_hbm.1, s32[2,128]{1,0:T(2,128)} %bitcast.17, bf16[2,128]{1,0:T(2,128)(2,1)} %bitcast.18, bf16[128,2048]{1,0:T(8,128)(2,1)} %tok_hbm.1, ...), custom_call_target="tpu_custom_call" | custom-call | flops 9059696640 | bytes 12582912 | tf_op jit(solution)/shard_map/moe_layer/pallas_call | solution.py:514
  91.5 2.1 %hand_over.1 = (bf16[128,2048]{1,0:T(8,128)(2,1)}, bf16[2,128]{1,0:T(2,128)(2,1)}, f32[64,768]{1,0:T(8,128)}, f32[64,768]{1,0:T(8,128)}, f32[64,768]{1,0:T(8,128)}) custom-call(bf16[128,2048]{1,0:T(8,128)(2,1)} %get-tuple-element.15.refs_0_, bf16[2,128]{1,0:T(2,128)(2,1)} %get-tuple-element.16.refs_1_, f32[64,768]{1,0:T(8,128)} %get-tuple-element.17.refs_2_, ...), custom_call_target="tpu_custom_call" | custom-call | tf_op jit(solution)/shard_map/hand_over/pallas_call | solution.py:584

commit v6 on v5

--- a/solution.py
+++ b/solution.py
@@ -404,21 +404,23 @@
         gg[:, cols] = (hg * act1[:, cols]).astype(BF16)
         ug[:, cols] = (hg * act2[:, cols]).astype(BF16)
 
+    def pair_cols(n):
+        cols = cols_at(n * 256, 256)
+        pair[:, cols] = (mm_nt(gg[...], wg[cols, :]) + mm_nt(ug[...], wu[cols, :])).astype(BF16)
+
     for m, right in ((1, gg), (2, ug)):
 
         @pl.loop(0, NZ)
         def _(s):
             put_grads(m, s, mm(turned[s], right[...]).astype(BF16))
 
+        if m == 2:
+            pl.loop(0, 2)(pair_cols)
         ring_step(m, 0)
         if m == 1:
             ring_step(0, ROUNDS - 1)
 
-    def pair_cols(n):
-        cols = cols_at(n * 256, 256)
-        pair[:, cols] = (mm_nt(gg[...], wg[cols, :]) + mm_nt(ug[...], wu[cols, :])).astype(BF16)
-
-    pl.loop(0, 8)(pair_cols)
+    pl.loop(2, 8)(pair_cols)
 
     @pl.loop(0, 2)
     def _(n):

time: 94.5 us -> 94.5 us (level)
  no operation moved by 1% of the time
where the time goes in v6:
time: 94.5 us; the launch traced here: 93.7 us
  Pallas kernels  93 us (98%)
    pallas_call x1, Pallas kernels, layer(): pl.pallas_call(layer_kernel, out_shape=shapes, in_specs=[anywhere] * 9, o...  90.9 us
    pallas_call x1, Pallas kernels, layer(): pl.pallas_call(hand_over, out_shape=shapes, in_specs=[anywhere] * 5, out_...  2.11 us

profile of v6, /device:TPU:24, one launch (start us, length us, event | category | flops | bytes accessed | tf_op | source)
XLA Modules:
  0.0 93.7 jit_solution(13438757982127862907)
XLA Ops:
  0.6 90.9 %moe_layer.1 = (bf16[128,2048]{1,0:T(8,128)(2,1)}, bf16[2,128]{1,0:T(2,128)(2,1)}, f32[64,768]{1,0:T(8,128)}, f32[64,768]{1,0:T(8,128)}, f32[64,768]{1,0:T(8,128)}) custom-call(s32[8]{0:T(128)} %slot_hbm.1, s32[2]{0:T(128)} %live_hbm.1, s32[2,128]{1,0:T(2,128)} %bitcast.17, bf16[2,128]{1,0:T(2,128)(2,1)} %bitcast.18, bf16[128,2048]{1,0:T(8,128)(2,1)} %tok_hbm.1, ...), custom_call_target="tpu_custom_call" | custom-call | flops 9059696640 | bytes 12582912 | tf_op jit(solution)/shard_map/moe_layer/pallas_call | solution.py:516
  91.5 2.1 %hand_over.1 = (bf16[128,2048]{1,0:T(8,128)(2,1)}, bf16[2,128]{1,0:T(2,128)(2,1)}, f32[64,768]{1,0:T(8,128)}, f32[64,768]{1,0:T(8,128)}, f32[64,768]{1,0:T(8,128)}) custom-call(bf16[128,2048]{1,0:T(8,128)(2,1)} %get-tuple-element.15.refs_0_, bf16[2,128]{1,0:T(2,128)(2,1)} %get-tuple-element.16.refs_1_, f32[64,768]{1,0:T(8,128)} %get-tuple-element.17.refs_2_, ...), custom_call_target="tpu_custom_call" | custom-call | tf_op jit(solution)/shard_map/hand_over/pallas_call | solution.py:586
